TPU v7x, 32 devices: a whole 2x2x4 slice. The times are simulated.
32 devices in a mesh: pair: 16 (over z, x, core), trow: 2 (over y).
Axes of the slice: x: 2, y: 2, z: 4, core: 2. Of those that a mesh axis runs over, the one named last changes fastest.
Arguments:
- query_bank: bfloat16 [16, 64, 1024], P('pair'), may hold values from -6 to 6
- ref_owner: int32 [1], replicated, may hold values from 0 to 15
- target_feat: bfloat16 [16, 512, 1024], P('pair', None, 'trow'), may hold values from -60 to 60
- valid_rows: int32 [16], P('pair'), may hold values from 2 to 16, as said below
- w_first: bfloat16 [16, 1, 3, 3, 3, 3], replicated, may hold values from -2 to 2
- b_first: float32 [16], replicated, may hold values from -0.5 to 0.5
- w_middle: bfloat16 [16, 16, 3, 3, 3, 3], replicated, may hold values from -0.25 to 0.25
- b_middle: float32 [16], replicated, may hold values from -0.5 to 0.5
- w_last: bfloat16 [1, 16, 3, 3, 3, 3], replicated, may hold values from -0.25 to 0.25
- b_last: float32 [1], replicated, may hold values from -0.5 to 0.5
Outputs:
- scores: float32 [16, 64, 512], P('pair', None, 'trow')
Inputs may be any that keep to these rules, and one draw needn't show every extreme that they name: ref_owner names the group along pair whose window is the reference. Rows of a target grid at or past valid_rows are padding; some pair fills all 16 rows.
All inputs are finite; a program needn't handle non-finite values.
Results may differ from a plain program's by a relative error of at most 0.007.
Values may be sent and summed in bfloat16 or wider, within the bound.
No kernel may reach another device: no remote copies, remote signals or barrier semaphores. Data moves between devices by JAX's collectives and lax.ppermute only.
A program may use at most 64 MiB of HBM per device.

v0:
```python
import math

import jax
import jax.numpy as jnp
from jax import lax
from jax.sharding import PartitionSpec as P

WB = 32
WA = 32


EPS_NORM = 1e-06
EPS_PEAK = 1e-05


def extended(cells, sides, width):
    for axis, dim in sides:
        count = lax.axis_size(axis)
        ends = count - 1
        head = lax.slice_in_dim(cells, 0, width, axis=dim)
        tail = lax.slice_in_dim(cells, cells.shape[dim] - width, cells.shape[dim], axis=dim)
        cells = jnp.concatenate(
            [
                lax.ppermute(tail, axis, [(i, (i + 1) % count) for i in range(ends)]),
                cells,
                lax.ppermute(head, axis, [((i + 1) % count, i) for i in range(ends)]),
            ],
            axis=dim,
        )
    return cells


def broadcast(shard, axis, root):
    mine = lax.axis_index(axis) == root
    return lax.psum(jnp.where(mine, shard, jnp.zeros_like(shard)), axis)


def shift_along(values, offset, axis_dim):
    if offset == 0:
        return values
    length = values.shape[axis_dim]
    zero_shape = list(values.shape)
    zero_shape[axis_dim] = abs(offset)
    zero_block = jnp.zeros(zero_shape, values.dtype)
    if offset > 0:
        return jnp.concatenate(
            [lax.slice_in_dim(values, offset, length, axis=axis_dim), zero_block], axis=axis_dim
        )
    return jnp.concatenate(
        [zero_block, lax.slice_in_dim(values, 0, length + offset, axis=axis_dim)], axis=axis_dim
    )


def block_conv(row_block, weight_matrix, out_channels, block_rows):
    extent = row_block.shape[2]
    column_pos = jnp.arange(extent, dtype=jnp.int32) % WB
    shifted = []
    for col_off in (-1, 0, 1):
        in_range = (column_pos + col_off >= 0) & (column_pos + col_off < WB)
        moved_cols = shift_along(row_block, col_off, 2)
        shifted.append(
            jnp.where(in_range[None, None, :], moved_cols, jnp.zeros((), row_block.dtype))
        )
    layers = []
    for row_off in range(3):
        for col_idx in range(3):
            layers.append(
                lax.slice_in_dim(
                    shifted[col_idx], row_off * WB, (row_off + block_rows) * WB, axis=2
                )
            )
    stacked = jnp.concatenate(layers, axis=0)
    products = jnp.einsum("pk,kab->pab", weight_matrix, stacked, preferred_element_type=jnp.float32)
    positions = row_block.shape[1]
    query_row = jnp.arange(positions, dtype=jnp.int32) // WA
    query_col = jnp.arange(positions, dtype=jnp.int32) % WA
    ref_rows = positions // WA
    accumulated = jnp.zeros((out_channels, positions, block_rows * WB), jnp.float32)
    for row_off in range(3):
        for col_off in range(3):
            start_chan = (row_off * 3 + col_off) * out_channels
            offset_group = products[start_chan : start_chan + out_channels]
            in_range = (query_row + row_off - 1 >= 0) & (query_row + row_off - 1 < ref_rows)
            in_range = in_range & (query_col + col_off - 1 >= 0) & (query_col + col_off - 1 < WA)
            moved_group = shift_along(offset_group, (row_off - 1) * WA + col_off - 1, 1)
            accumulated = accumulated + jnp.where(in_range[None, :, None], moved_group, 0.0)
    return accumulated


def conv_layer(inputs, weight, bias):
    out_channels = weight.shape[0]
    in_channels = weight.shape[1]
    weight_matrix = jnp.transpose(weight, (2, 3, 0, 4, 5, 1)).reshape(
        9 * out_channels, 9 * in_channels
    )
    rows_out = inputs.shape[2] // WB - 2
    block_rows = 1
    for option in (2, 4):
        block_rows = option

    def one_block(block_index):
        row_block = lax.dynamic_slice_in_dim(
            inputs, block_index * (block_rows * WB), (block_rows + 2) * WB, 2
        )
        return block_conv(row_block, weight_matrix, out_channels, block_rows)

    block_outputs = lax.map(one_block, jnp.arange(rows_out // block_rows, dtype=jnp.int32))
    joined = jnp.transpose(block_outputs, (1, 2, 0, 3)).reshape(
        out_channels, inputs.shape[1], rows_out * WB
    )
    return joined + bias[:, None, None]


def unit_rows(features):
    values = features.astype(jnp.float32)
    return (values * lax.rsqrt(jnp.sum(values * values, axis=1, keepdims=True) + EPS_NORM)).astype(
        jnp.bfloat16
    )


def contract(left, right):
    return lax.dot_general(
        left, right, (((1,), (1,)), ((), ())), preferred_element_type=jnp.float32
    )


def score_pair(raw_dot, squares, trow_rank, row_count, cos_scale, weights):
    w_first, b_first, w_middle, b_middle, w_last, b_last = weights
    rows_here = raw_dot.shape[1] // WB
    first_row = trow_rank * rows_here
    global_row = first_row + jnp.arange(raw_dot.shape[1], dtype=jnp.int32) // WB
    is_live = global_row < row_count
    correlation = jnp.where(
        is_live[None, :], cos_scale * raw_dot * lax.rsqrt(squares + EPS_NORM)[None, :], 0.0
    )
    magnitude = jnp.abs(correlation)
    peak_query = jnp.max(magnitude, axis=0)
    peak_target = lax.pmax(jnp.max(magnitude, axis=1), "trow")
    volume = (
        correlation
        * (correlation / (peak_query[None, :] + EPS_PEAK))
        * (correlation / (peak_target[:, None] + EPS_PEAK))
    )
    volume = volume.astype(jnp.bfloat16)[None]
    padded = extended(volume, (("trow", 2),), WB)
    hidden = jnp.maximum(conv_layer(padded, w_first, b_first), 0.0).astype(jnp.bfloat16)
    padded = extended(hidden, (("trow", 2),), WB)
    hidden = jnp.maximum(conv_layer(padded, w_middle, b_middle), 0.0).astype(jnp.bfloat16)
    padded = extended(hidden, (("trow", 2),), WB)
    result = conv_layer(padded, w_last, b_last)[0]
    return jnp.where(is_live[None, :], result, 0.0)


def per_device(
    query_bank,
    ref_owner,
    target_feat,
    valid_rows,
    w_first,
    b_first,
    w_middle,
    b_middle,
    w_last,
    b_last,
):
    query_vec = broadcast(query_bank[0], "pair", ref_owner[0])
    unit_query = unit_rows(query_vec)
    cos_scale = math.sqrt(query_vec.shape[1])
    trow_rank = lax.axis_index("trow")
    weights = (w_first, b_first, w_middle, b_middle, w_last, b_last)
    exchanged = lax.all_to_all(target_feat, "trow", split_axis=1, concat_axis=2, tiled=True)
    local_rows = exchanged[0]
    raw_dot = contract(unit_query, local_rows)
    squares = jnp.sum(jnp.square(local_rows.astype(jnp.float32)), axis=1)
    scores = [score_pair(raw_dot, squares, trow_rank, valid_rows[0], cos_scale, weights)]
    return jnp.stack(scores)


def solution(mesh):
    in_specs = (
        P("pair", None, None),
        P(),
        P("pair", None, "trow"),
        P("pair"),
        P(),
        P(),
        P(),
        P(),
        P(),
        P(),
    )
    out_specs = P("pair", None, "trow")
    return jax.shard_map(
        per_device, mesh=mesh, in_specs=in_specs, out_specs=out_specs, check_vma=False
    )
```

profile of v0, /device:TPU:0, one launch (start us, length us, event | category | flops | bytes accessed | tf_op | source)
XLA Modules:
  0.0 179.3 jit_solution(13388305223076636024)
XLA Ops:
  7.2 1.6 select_bitcast_fusion
  8.8 1.9 %copy.50 = bf16[1,512,512]{2,0,1:T(2,128)(2,1)S(1)} copy(bf16[1,512,512]{2,1,0:T(8,128)(2,1)} %param.18) | data formatting | bytes 1048576 | tf_op args[2]
  10.6 0.5 broadcast.3951
  11.2 3.8 %reduce.1 = bf16[512,512]{1,0:T(8,128)(2,1)S(1)} reduce(bf16[512,1,512]{2,1,0:T(2,128)(2,1)S(1)} %bitcast.115, bf16[]{:T(256)} %broadcast.3951), dimensions={1}, to_apply=%bitcast.78.reduce_sub_computation | reduce | bytes 1048578
  15.0 1.1 reshape.509
  16.1 4.2 %all-to-all-start = ((bf16[2,2,65536]{2,1,0:T(2,128)(2,1)}), bf16[2,2,65536]{2,1,0:T(2,128)(2,1)S(1)}, u32[]{:S(2)}, u32[]{:S(2)}) async-start(bf16[2,2,65536]{2,1,0:T(2,128)(2,1)} %reshape.509), calls=%async_computation | async-start | bytes 1048576 | tf_op jit(solution)/shard_map/all_to_all | solution.py:171
  21.0 79.5 %all-reduce.32.cloned.1.call-done = bf16[64,1024]{1,0:T(8,128)(2,1)} async-done(((bf16[64,1024]{1,0:T(8,128)(2,1)}), bf16[64,1024]{1,0:T(8,128)(2,1)}) %all-reduce.32.cloned.1.call-update) | async-done | bytes 131088 | tf_op jit(solution)/shard_map/psum | solution.py:35
  100.5 1.0 fusion.30
  101.6 0.5 reshape.510
  102.2 0.2 copy.31
  102.6 0.3 abs_reduce_fusion.1
  103.0 4.9 %pmax.7 = f32[64]{0:T(128)S(1)} all-reduce(f32[64]{0:T(128)S(1)} %get-tuple-element.455), channel_id=1, replica_groups=mesh['pair'=16,'trow'=2] {'trow'}, use_global_device_ids=true, to_apply=%region_5.6 | all-reduce | flops 64 | bytes 512 | tf_op jit(solution)/shard_map/pmax | solution.py:138
  108.1 3.4 %collective-permute-start = (bf16[1,64,32]{2,1,0:T(8,128)(2,1)S(1)}, bf16[1,64,32]{2,1,0:T(8,128)(2,1)S(1)}, u32[]{:S(2)}, u32[]{:S(2)}) collective-permute-start(bf16[1,64,32]{2,1,0:T(8,128)(2,1)S(1)} %get-tuple-element.560), channel_id=1, source_target_pairs={{0,1},{2,3},{4,5},{6,7},{8,9},{10,11},{12,13},{14,15},{16,17},{18,... | collective-permute-start | bytes 12296 | tf_op jit(solution)/shard_map/ppermute | solution.py:24
  111.5 1.3 collective-permute-start.1
  112.9 4.2 %collective-permute-done.1 = bf16[1,64,32]{2,1,0:T(8,128)(2,1)S(1)} collective-permute-done((bf16[1,64,32]{2,1,0:T(8,128)(2,1)S(1)}, bf16[1,64,32]{2,1,0:T(8,128)(2,1)S(1)}, u32[]{:S(2)}, u32[]{:S(2)}) %collective-permute-start.1) | collective-permute-done | bytes 4128 | tf_op jit(solution)/shard_map/ppermute | solution.py:26
  117.3 10.4 %while.45 = (s32[]{:T(128)}, f32[2,16,64,128]{3,1,2,0:T(8,128)S(1)}, s32[2]{0:T(128)S(1)}, bf16[1,64,320]{2,1,0:T(8,128)(2,1)S(1)}, bf16[144,9]{0,1:T(8,128)(2,1...) while((s32[]{:T(128)}, f32[2,16,64,128]{3,1,2,0:T(8,128)S(1)}, s32[2]{0:T(128)S(1)}, ...), condition=%wide.region_7.8_spmd, body=%wide.region_6.7_spmd.sunk | while | flops 23512260 | bytes 14720639 | solution.py:107
  117.3 0.6 dynamic_slice.71
  119.0 0.3 fusion.92
  119.6 0.5 concatenate.223
  120.1 0.8 convolution_bitcast_fusion.6
  121.2 1.2 fusion.97
  122.5 0.6 dynamic_slice.71
  124.2 0.3 fusion.92
  124.8 0.5 concatenate.223
  125.3 0.8 convolution_bitcast_fusion.6
  126.4 1.2 fusion.97
  128.0 1.6 collective-permute-start.2
  129.6 1.5 collective-permute-start.3
  131.3 0.2 reshape.503
  131.6 1.9 %collective-permute-done.2 = bf16[16,64,32]{2,0,1:T(8,128)(2,1)S(1)} collective-permute-done((bf16[16,64,32]{2,0,1:T(8,128)(2,1)S(1)}, bf16[16,64,32]{2,0,1:T(8,128)(2,1)S(1)}, u32[]{:S(2)}, u32[]{:S(2)}) %collective-permute-start.2) | collective-permute-done | bytes 65568 | tf_op jit(solution)/shard_map/ppermute | solution.py:24
  133.5 4.4 %collective-permute-done.3 = bf16[16,64,32]{2,0,1:T(8,128)(2,1)S(1)} collective-permute-done((bf16[16,64,32]{2,0,1:T(8,128)(2,1)S(1)}, bf16[16,64,32]{2,0,1:T(8,128)(2,1)S(1)}, u32[]{:S(2)}, u32[]{:S(2)}) %collective-permute-start.3) | collective-permute-done | bytes 65568 | tf_op jit(solution)/shard_map/ppermute | solution.py:26
  137.9 0.5 pad_maximum_fusion
  138.5 11.8 %while.46 = (s32[]{:T(128)}, f32[2,16,64,128]{3,1,2,0:T(8,128)S(1)}, s32[2]{0:T(128)S(1)}, bf16[16,64,320]{2,0,1:T(8,128)(2,1)S(1)}, bf16[144,144]{1,0:T(8,128)(...) while((s32[]{:T(128)}, f32[2,16,64,128]{3,1,2,0:T(8,128)S(1)}, s32[2]{0:T(128)S(1)}, ...), condition=%wide.region_9.10_spmd, body=%wide.region_8.9_spmd.sunk | while | flops 342569024 | bytes 24628092 | solution.py:107
  138.5 0.6 dynamic_slice.73
  139.7 0.5 constant_dynamic-slice_fusion.9
  140.2 0.2 pad_select_fusion.8
  140.5 0.2 dynamic-slice_select_fusion.4
  142.1 0.8 convolution_bitcast_fusion.7
  143.2 1.2 fusion.104
  144.4 0.6 dynamic_slice.73
  145.7 0.4 constant_dynamic-slice_fusion.9
  146.1 0.2 pad_select_fusion.8
  146.4 0.2 dynamic-slice_select_fusion.4
  148.0 0.8 convolution_bitcast_fusion.7
  149.1 1.2 fusion.104
  150.6 1.5 collective-permute-start.4
  152.1 1.3 collective-permute-start.5
  154.2 1.8 collective-permute-done.4
  156.0 4.4 %collective-permute-done.5 = bf16[16,64,32]{2,0,1:T(8,128)(2,1)S(1)} collective-permute-done((bf16[16,64,32]{2,0,1:T(8,128)(2,1)S(1)}, bf16[16,64,32]{2,0,1:T(8,128)(2,1)S(1)}, u32[]{:S(2)}, u32[]{:S(2)}) %collective-permute-start.5) | collective-permute-done | bytes 65568 | tf_op jit(solution)/shard_map/ppermute | solution.py:26
  160.4 0.5 pad_maximum_fusion.1
  160.9 10.9 %while.47 = (s32[]{:T(128)}, f32[2,1,64,128]{3,2,1,0:T(8,128)S(1)}, s32[2]{0:T(128)S(1)}, bf16[16,64,320]{2,0,1:T(8,128)(2,1)S(1)}, bf16[9,144]{1,0:T(8,128)(2,1...) while((s32[]{:T(128)}, f32[2,1,64,128]{3,2,1,0:T(8,128)S(1)}, s32[2]{0:T(128)S(1)}, ...), condition=%wide.region_11.12_spmd, body=%wide.region_10.11_spmd.sunk | while | flops 21975112 | bytes 11917275 | solution.py:107
  160.9 0.6 dynamic_slice.75
  162.0 0.4 constant_dynamic-slice_fusion.10
  162.5 0.2 pad_select_fusion.10
  162.8 0.2 dynamic-slice_select_fusion.5
  164.4 0.4 convolution_bitcast_fusion.8
  165.0 1.3 fusion.111
  166.4 0.6 dynamic_slice.75
  167.5 0.4 constant_dynamic-slice_fusion.10
  168.0 0.2 pad_select_fusion.10
  168.3 0.2 dynamic-slice_select_fusion.5
  169.8 0.4 convolution_bitcast_fusion.8
  170.5 1.3 fusion.111
  171.8 0.6 bitcast_select_fusion
  (166 shorter events, 10.0 us)
Async XLA Ops:
  6.5 94.0 %all-reduce.32.cloned.1.call-start = ((), (), s32[]{:S(2)}) async-start(), calls=%async_computation.1 | async-start | bytes 262144 | tf_op jit(solution)/shard_map/psum | solution.py:35
  16.1 85.5 %all-to-all-start = ((bf16[2,2,65536]{2,1,0:T(2,128)(2,1)}), bf16[2,2,65536]{2,1,0:T(2,128)(2,1)S(1)}, u32[]{:S(2)}, u32[]{:S(2)}) async-start(bf16[2,2,65536]{2,1,0:T(2,128)(2,1)} %reshape.509), calls=%async_computation | async-start | bytes 1048576 | tf_op jit(solution)/shard_map/all_to_all | solution.py:171
  101.5 1.1 copy-start
  102.1 10.7 %copy-start.2 = (bf16[16,1,3,3,3,3]{0,5,4,3,2,1:T(4,128)(2,1)S(1)}, bf16[16,1,3,3,3,3]{0,5,4,3,2,1:T(4,128)(2,1)}, u32[]{:S(2)}) copy-start(bf16[16,1,3,3,3,3]{0,5,4,3,2,1:T(4,128)(2,1)} %param.20) | copy-start | bytes 7780
  108.1 4.8 %collective-permute-start = (bf16[1,64,32]{2,1,0:T(8,128)(2,1)S(1)}, bf16[1,64,32]{2,1,0:T(8,128)(2,1)S(1)}, u32[]{:S(2)}, u32[]{:S(2)}) collective-permute-start(bf16[1,64,32]{2,1,0:T(8,128)(2,1)S(1)} %get-tuple-element.560), channel_id=1, source_target_pairs={{0,1},{2,3},{4,5},{6,7},{8,9},{10,11},{12,13},{14,15},{16,17},{18,... | collective-permute-start | bytes 12296 | tf_op jit(solution)/shard_map/ppermute | solution.py:24
  111.5 5.6 %collective-permute-start.1 = (bf16[1,64,32]{2,1,0:T(8,128)(2,1)S(1)}, bf16[1,64,32]{2,1,0:T(8,128)(2,1)S(1)}, u32[]{:S(2)}, u32[]{:S(2)}) collective-permute-start(bf16[1,64,32]{2,1,0:T(8,128)(2,1)S(1)} %get-tuple-element.561), channel_id=1, source_target_pairs={{1,0},{3,2},{5,4},{7,6},{9,8},{11,10},{13,12},{15,14},{17,16},{19,... | collective-permute-start | bytes 12296 | tf_op jit(solution)/shard_map/ppermute | solution.py:26
  117.3 10.4 %copy-start.4 = (f32[16]{0:T(128)S(1)}, f32[16]{0:T(128)}, u32[]{:S(2)}) copy-start(f32[16]{0:T(128)} %param.21) | copy-start | bytes 196
  127.7 3.5 %copy-start.1 = (bf16[16,16,3,3,3,3]{1,0,5,4,3,2:T(8,128)(2,1)S(1)}, bf16[16,16,3,3,3,3]{1,0,5,4,3,2:T(8,128)(2,1)}, u32[]{:S(2)}) copy-start(bf16[16,16,3,3,3,3]{1,0,5,4,3,2:T(8,128)(2,1)} %param.22) | copy-start | bytes 124420
  128.0 5.5 %collective-permute-start.2 = (bf16[16,64,32]{2,0,1:T(8,128)(2,1)S(1)}, bf16[16,64,32]{2,0,1:T(8,128)(2,1)S(1)}, u32[]{:S(2)}, u32[]{:S(2)}) collective-permute-start(bf16[16,64,32]{2,0,1:T(8,128)(2,1)S(1)} %get-tuple-element.558), channel_id=1, source_target_pairs={{0,1},{2,3},{4,5},{6,7},{8,9},{10,11},{12,13},{14,15},{16,17},{18,... | collective-permute-start | bytes 196616 | tf_op jit(solution)/shard_map/ppermute | solution.py:24
  129.6 8.3 %collective-permute-start.3 = (bf16[16,64,32]{2,0,1:T(8,128)(2,1)S(1)}, bf16[16,64,32]{2,0,1:T(8,128)(2,1)S(1)}, u32[]{:S(2)}, u32[]{:S(2)}) collective-permute-start(bf16[16,64,32]{2,0,1:T(8,128)(2,1)S(1)} %get-tuple-element.559), channel_id=1, source_target_pairs={{1,0},{3,2},{5,4},{7,6},{9,8},{11,10},{13,12},{15,14},{17,16},{19,... | collective-permute-start | bytes 196616 | tf_op jit(solution)/shard_map/ppermute | solution.py:26
  138.5 11.8 %copy-start.5 = (f32[16]{0:T(128)S(1)}, f32[16]{0:T(128)}, u32[]{:S(2)}) copy-start(f32[16]{0:T(128)} %param.23) | copy-start | bytes 196
  150.3 3.1 %copy-start.3 = (bf16[1,16,3,3,3,3]{1,5,4,3,2,0:T(4,128)(2,1)S(1)}, bf16[1,16,3,3,3,3]{1,5,4,3,2,0:T(4,128)(2,1)}, u32[]{:S(2)}) copy-start(bf16[1,16,3,3,3,3]{1,5,4,3,2,0:T(4,128)(2,1)} %param.24) | copy-start | bytes 7780
  150.6 5.3 %collective-permute-start.4 = (bf16[16,64,32]{2,0,1:T(8,128)(2,1)S(1)}, bf16[16,64,32]{2,0,1:T(8,128)(2,1)S(1)}, u32[]{:S(2)}, u32[]{:S(2)}) collective-permute-start(bf16[16,64,32]{2,0,1:T(8,128)(2,1)S(1)} %get-tuple-element.556), channel_id=1, source_target_pairs={{0,1},{2,3},{4,5},{6,7},{8,9},{10,11},{12,13},{14,15},{16,17},{18,... | collective-permute-start | bytes 196616 | tf_op jit(solution)/shard_map/ppermute | solution.py:24
  152.1 8.3 %collective-permute-start.5 = (bf16[16,64,32]{2,0,1:T(8,128)(2,1)S(1)}, bf16[16,64,32]{2,0,1:T(8,128)(2,1)S(1)}, u32[]{:S(2)}, u32[]{:S(2)}) collective-permute-start(bf16[16,64,32]{2,0,1:T(8,128)(2,1)S(1)} %get-tuple-element.557), channel_id=1, source_target_pairs={{1,0},{3,2},{5,4},{7,6},{9,8},{11,10},{13,12},{15,14},{17,16},{19,... | collective-permute-start | bytes 196616 | tf_op jit(solution)/shard_map/ppermute | solution.py:26
Sparse Core Ops, SparseCore 0:
  10.8 89.6 all-reduce.31
where the time goes:
time: 181 us; the launch traced here: 179 us
  waiting for transfers between devices  96.2 us (53%)
  other arithmetic  19.7 us (11%)
  local copies, waits for them, and re-layouts  19 us (10%)
  between operations  15.7 us (9%)
  starting transfers between devices  14.8 us (8%)
  blocking collectives  4.94 us (3%)
  loops' own time  4.64 us (3%)
  matrix products  4.31 us (2%)
    psum x1, waiting for transfers between devices, broadcast(): return lax.psum(jnp.where(mine, shard, jnp.zeros_like(shard)), axis)  79.5 us
    ppermute x3, waiting for transfers between devices, extended(): lax.ppermute(head, axis, [((i + 1) % count, i) for i in range(ends)])  13 us
    ppermute x3, starting transfers between devices, extended(): lax.ppermute(tail, axis, [(i, (i + 1) % count) for i in range(ends)])  6.49 us
    dynamic_update_slice x4, other arithmetic, conv_layer(): lax.map(one_block, jnp.arange(rows_out // block_rows, dtype=jnp.int32))  4.99 us
    pmax x1, blocking collectives, score_pair(): peak_target = lax.pmax(jnp.max(magnitude, axis=1), 'trow')  4.94 us
    another operation x3, loops' own time, conv_layer(): lax.map(one_block, jnp.arange(rows_out // block_rows, dtype=jnp.int32))  4.64 us
    while x36, local copies, waits for them, and re-layouts  4.33 us
    all_to_all x1, starting transfers between devices, per_device(): lax.all_to_all(target_feat, 'trow', split_axis=1, concat_axis=2, tiled=True)  4.23 us
  transfers between devices with their start and end apart: 8, of which 6 were waited for; matrix products, arithmetic and copies ran while one was open for 5% of the time, Pallas kernels for 0%

commit v1 on v0

v1 whole, which is shorter than its diff:
```python
import functools
import math

import jax
import jax.numpy as jnp
from jax import lax
from jax.experimental import pallas as pl
from jax.experimental.pallas import tpu as pltpu
from jax.sharding import PartitionSpec as P

WB = 32
WA = 32

EPS_NORM = 1e-06
EPS_PEAK = 1e-05

F32 = jnp.float32
BF16 = jnp.bfloat16
NT = (((1,), (1,)), ((), ()))
PITCH = WB + 8
VMEM_LIMIT = 48 * 1024 * 1024


def swapped(values, axis, distance):
    count = lax.axis_size(axis)
    return lax.ppermute(values, axis, [(i, i ^ distance) for i in range(count)])


def spread(window, owner, axis):
    count = lax.axis_size(axis)
    rank = lax.axis_index(axis)
    held = jnp.where(rank == owner, window, jnp.zeros_like(window))
    half = window.shape[0] // 2
    bit = rank % 2
    keep = lax.dynamic_slice_in_dim(held, bit * half, half, 0)
    give = lax.dynamic_slice_in_dim(held, (1 - bit) * half, half, 0)
    held = keep + swapped(give, axis, 1)
    bits = [1 << b for b in range(1, count.bit_length() - 1)]
    rounds = []
    if len(bits) % 2:
        rounds.append(bits[:1])
        bits = bits[1:]
    for at in range(0, len(bits), 2):
        low, high = bits[at : at + 2]
        rounds.append([low, high, low + high])
    for distances in rounds:
        held = held + sum(swapped(held, axis, d) for d in distances)
    return held, swapped(held, axis, 1)


def dot(left, right):
    return jnp.dot(left, right, preferred_element_type=F32)


def dot_nt(left, right):
    return lax.dot_general(left, right, NT, preferred_element_type=F32)


def iota(shape, dim):
    return lax.broadcasted_iota(jnp.int32, shape, dim)


def one_hot(cond):
    return jnp.where(cond, 1.0, 0.0).astype(BF16)


def expand_kernel(ch, wf_ref, wm_ref, wl_ref, w1_ref, w2_ref, w3_ref):
    group = 2 * ch
    index = lambda i, j, k, l: ((i * 3 + j) * 3 + k) * 3 + l

    taps = wf_ref[...]
    lane = iota((81, 128), 1)
    src = iota((81, 128), 0)
    base = []
    for k in range(3):
        for ra in range(2):
            l, rp, j = lane // 6, (lane // 3) % 2, lane % 3
            want = (((rp - ra + 1) * 3 + j) * 3 + k) * 3 + l
            base.append(dot(taps, one_hot((src == want) & (lane < 18))))
    base = jnp.concatenate(base, axis=0).astype(BF16)
    row = iota((128, 256), 0)
    col = iota((128, 256), 1)
    l, rp, j = row // 6, (row // 3) % 2, row % 3
    for ca in range(WA):
        at = ca + j - 1
        place = one_hot((col == l * 64 + rp * WA + at) & (at >= 0) & (at < WA) & (row < 18))
        block = dot(base, place).astype(BF16)
        for k in range(3):
            w1_ref[k, ca * group : (ca + 1) * group, :] = block[k * group : (k + 1) * group]

    total = None
    row = iota((ch, 128), 0)
    col = iota((ch, 128), 1)
    for j in range(3):
        for rp in range(2):
            picked = jnp.concatenate(
                [wm_ref[index(rp - ra + 1, j, k, l)] for k in range(3) for l in range(3) for ra in range(2)],
                axis=0,
            )
            part = dot(picked, one_hot(col == j * group + rp * ch + row))
            total = part if total is None else total + part
    base = total.astype(BF16)
    row = iota((128, 256), 0)
    col = iota((128, 256), 1)
    moves = [one_hot((col == row + group * b) & (row < 3 * group)) for b in range(4)]
    moved = [dot(base, m).astype(BF16) for m in moves]
    blank = jnp.zeros((group, 128), BF16)
    for tap in range(9):
        for ca in range(8):
            a, b = divmod(ca + 3, 4)
            piece = moved[b][tap * group : (tap + 1) * group]
            for v in range(4):
                chunk = piece[:, :128] if v == a else piece[:, 128:] if v == a + 1 else blank
                w2_ref[tap, ca * group : (ca + 1) * group, v * 128 : (v + 1) * 128] = chunk

    taps = wl_ref[...]
    out_row = iota((24, 81), 0)
    src = iota((24, 81), 1)
    row = iota((ch, 128), 0)
    col = iota((ch, 128), 1)
    total = None
    for j in range(3):
        for rp in range(2):
            k, l, ra = out_row // 8, (out_row % 8) // 2, out_row % 2
            want = (((rp - ra + 1) * 3 + j) * 3 + k) * 3 + l
            picked = dot(one_hot((src == want) & (l < 3)), taps).astype(BF16)
            part = dot(picked, one_hot(col == j * group + rp * ch + row))
            total = part if total is None else total + part
    base = total.astype(BF16)
    moved = [dot(base, m) for m in moves]
    blank = jnp.zeros((8, 128), F32)
    lanes = WA * group // 128
    for k in range(3):
        for pair in range(WA // 2):
            for v in range(lanes):
                chunks = []
                for ca in (2 * pair, 2 * pair + 1):
                    a, b = (ca - 1) // 4, (ca - 1) % 4
                    piece = moved[b][k * 8 : (k + 1) * 8]
                    chunks.append(piece[:, :128] if v == a else piece[:, 128:] if v == a + 1 else blank)
                w3_ref[k, pair * 16 : (pair + 1) * 16, v * 128 : (v + 1) * 128] = jnp.concatenate(
                    chunks, axis=0
                ).astype(BF16)


def score_kernel(
    rows_here, n1, n2, s_ref, b3_ref, tm_ref, to_ref, qa_ref, qb_ref, w1_ref, w2_ref, w3_ref, b1_ref, b2_ref,
    out_ref, v_ref, x_ref, h1_ref, h2_ref, ya_ref, yb_ref, yt_ref,
):
    count, trow, bit = s_ref[0], s_ref[1], s_ref[2]
    cells = tm_ref.shape[0]
    grid_rows = cells // WB
    width = tm_ref.shape[1]
    scale = math.sqrt(2 * width)
    start1 = jnp.clip(rows_here * trow - 2, 0, grid_rows - n1)
    start2 = jnp.clip(rows_here * trow - 1, 0, grid_rows - n2)

    def unit(ref):
        values = ref[...].astype(F32)
        return (values * lax.rsqrt(jnp.sum(values * values, axis=1, keepdims=True) + EPS_NORM)).astype(BF16)

    qa, qb = unit(qa_ref), unit(qb_ref)
    own_first = bit == 0
    q0 = jnp.where(own_first, qa, qb)
    q1 = jnp.where(own_first, qb, qa)
    query = jnp.concatenate([q0, q1, q0, q1], axis=0)
    low, high = query[:, :width], query[:, width:]
    near = jnp.where(trow == 0, low, high)
    far = jnp.where(trow == 0, high, low)
    raw = dot_nt(tm_ref[...], near) + dot_nt(to_ref[...], far)

    def squares(ref):
        values = ref[...].astype(F32)
        return jnp.sum(values * values, axis=1, keepdims=True)

    inv = lax.rsqrt(squares(tm_ref) + squares(to_ref) + EPS_NORM)
    live = iota((cells, 128), 0) // WB < count
    corr = jnp.where(live, scale * raw * inv, 0.0)
    mag = jnp.abs(corr)
    peak_query = jnp.max(mag, axis=1, keepdims=True)
    peak_target = jnp.max(mag, axis=0, keepdims=True)
    volume = corr * (corr * (1.0 / (peak_query + EPS_PEAK))) * (corr * (1.0 / (peak_target + EPS_PEAK)))

    v_ref[0 : 8 + PITCH, :] = jnp.zeros((8 + PITCH, 128), F32)
    v_ref[8 + (grid_rows + 1) * PITCH :, :] = jnp.zeros((PITCH, 128), F32)
    for r in range(grid_rows):
        at = 8 + (r + 1) * PITCH
        v_ref[at : at + WB, :] = volume[r * WB : (r + 1) * WB]
        v_ref[at + WB : at + PITCH, :] = jnp.zeros((PITCH - WB, 128), F32)

    half = WB // 2
    left = iota((half, 128), 1) < 64
    for r in range(n1 + 2):
        at = pl.multiple_of((start1 + r) * PITCH, 8)
        slabs = [v_ref[pl.ds(at + 8 + o, half, stride=2), :] for o in (-1, 0, 1, 2)]
        for u in range(2):
            x_ref[r, u * half : (u + 1) * half, 0:128] = jnp.where(left, slabs[u], slabs[u + 1]).astype(BF16)
            x_ref[r, u * half : (u + 1) * half, 128:256] = jnp.where(left, slabs[u + 2], 0.0).astype(BF16)

    lanes = h1_ref.shape[2]
    zero = jnp.zeros((2 * WB, lanes), BF16)
    h1_ref[0] = zero
    h1_ref[n1 + 1] = zero
    h2_ref[0] = zero[:WB]
    h2_ref[n2 + 1] = zero[:WB]
    step = iota((n1 * half, 256), 0) % half
    for q in range(lanes // 256):
        cols = slice(q * 256, (q + 1) * 256)
        total = b1_ref[:, cols]
        for k in range(3):
            total = total + dot_nt(x_ref[k : k + n1].reshape(n1 * WB, 256), w1_ref[k, cols, :])
        total = jnp.maximum(total, 0.0)
        h1_ref[1 : n1 + 1, half : half + WB, cols] = total.reshape(n1, WB, 256).astype(BF16)
        parts = total.reshape(n1, 2, half, 256)
        even = parts[:, 0].reshape(n1 * half, 256)
        odd = parts[:, 1].reshape(n1 * half, 256)
        before = jnp.where(step == 0, 0.0, pltpu.roll(odd, 1, 0))
        after = jnp.where(step == half - 1, 0.0, pltpu.roll(even, n1 * half - 1, 0))
        h1_ref[1 : n1 + 1, 0:half, cols] = before.reshape(n1, half, 256).astype(BF16)
        h1_ref[1 : n1 + 1, half + WB :, cols] = after.reshape(n1, half, 256).astype(BF16)

    off2 = start2 - start1
    for q in range(lanes // 256):
        cols = slice(q * 256, (q + 1) * 256)
        lo, hi = max(q * 256 - 128, 0), min(q * 256 + 384, lanes)
        total = b2_ref[:, cols]
        for k in range(3):
            for l in range(3):
                cells_in = h1_ref[pl.ds(off2 + k, n2), l * half : l * half + WB, lo:hi].reshape(n2 * WB, hi - lo)
                total = total + dot_nt(cells_in, w2_ref[k * 3 + l, :, lo - q * 256 + 128 : hi - q * 256 + 128])
        h2_ref[1 : n2 + 1, :, cols] = jnp.maximum(total, 0.0).reshape(n2, WB, 256).astype(BF16)

    off3 = rows_here * trow - start2
    total = None
    for k in range(3):
        part = dot_nt(h2_ref[pl.ds(off3 + k, rows_here)].reshape(rows_here * WB, lanes), w3_ref[k])
        total = part if total is None else total + part
    for r in range(rows_here):
        for u in range(2):
            piece = total[(r * 2 + u) * half : (r * 2 + u + 1) * half]
            ya_ref[pl.ds(r * WB + u, half, stride=2), :] = piece[:, :128]
            yb_ref[pl.ds(r * WB + u, half, stride=2), :] = piece[:, 128:]
    here = rows_here * WB
    for v in range(here // 128):
        yt_ref[v, 0:128, :] = ya_ref[v * 128 : (v + 1) * 128, :].T
        yt_ref[v, 128:256, :] = yb_ref[v * 128 : (v + 1) * 128, :].T
    lane = iota((WA, here), 1)
    keep = rows_here * trow + lane // WB < count
    for ra in range(2):
        parts = [
            jnp.concatenate([yt_ref[v, pl.ds(l * 2 + ra, WA, stride=8), :] for v in range(here // 128)], axis=1)
            for l in range(3)
        ]
        before = jnp.where(lane % WB == 0, 0.0, pltpu.roll(parts[0], 1, 1))
        after = jnp.where(lane % WB == WB - 1, 0.0, pltpu.roll(parts[2], here - 1, 1))
        result = before + parts[1] + after + b3_ref[0]
        out_ref[0, ra * WA : (ra + 1) * WA, :] = jnp.where(keep, result, 0.0)


def per_device(
    query_bank, ref_owner, target_feat, valid_rows, w_first, b_first, w_middle, b_middle, w_last, b_last
):
    target = target_feat[0]
    cells, width = target.shape
    positions = query_bank.shape[1]
    ch = w_middle.shape[0]
    group = 2 * ch
    lanes = WA * group
    trows = lax.axis_size("trow")
    grid_rows = cells // WB
    rows_here = grid_rows // trows
    sides = 1 if trows == 2 else 2
    n1, n2 = min(rows_here + 2 * sides, grid_rows), min(rows_here + sides, grid_rows)

    other = swapped(target, "trow", 1)
    own, sibling = spread(query_bank[0], ref_owner[0], "pair")
    scalars = jnp.stack([valid_rows[0], lax.axis_index("trow"), lax.axis_index("pair") % 2]).astype(jnp.int32)

    vmem = pl.BlockSpec(memory_space=pltpu.VMEM)
    smem = pl.BlockSpec(memory_space=pltpu.SMEM)
    w1, w2, w3 = pl.pallas_call(
        functools.partial(expand_kernel, ch),
        out_shape=(
            jax.ShapeDtypeStruct((3, lanes, 256), BF16),
            jax.ShapeDtypeStruct((9, 256, 512), BF16),
            jax.ShapeDtypeStruct((3, 256, lanes), BF16),
        ),
        in_specs=[vmem] * 3,
        out_specs=(vmem,) * 3,
        compiler_params=pltpu.CompilerParams(vmem_limit_bytes=VMEM_LIMIT),
        name="expand",
    )(
        w_first.reshape(ch, 81),
        jnp.transpose(w_middle, (2, 3, 4, 5, 0, 1)).reshape(81, ch, ch),
        jnp.transpose(w_last[0], (1, 2, 3, 4, 0)).reshape(81, ch),
    )
    b1 = jnp.tile(b_first, lanes // ch)[None]
    b2 = jnp.tile(b_middle, lanes // ch)[None]

    return pl.pallas_call(
        functools.partial(score_kernel, rows_here, n1, n2),
        out_shape=jax.ShapeDtypeStruct((1, positions, rows_here * WB), F32),
        in_specs=[smem, smem] + [vmem] * 9,
        out_specs=vmem,
        scratch_shapes=[
            pltpu.VMEM((8 + (grid_rows + 2) * PITCH, 128), F32),
            pltpu.VMEM((n1 + 2, WB, 256), BF16),
            pltpu.VMEM((n1 + 2, 2 * WB, lanes), BF16),
            pltpu.VMEM((n2 + 2, WB, lanes), BF16),
            pltpu.VMEM((rows_here * WB, 128), F32),
            pltpu.VMEM((rows_here * WB, 128), F32),
            pltpu.VMEM((rows_here * WB // 128, 256, 128), F32),
        ],
        compiler_params=pltpu.CompilerParams(vmem_limit_bytes=VMEM_LIMIT),
        name="score",
    )(scalars, b_last, target, other, own, sibling, w1, w2, w3, b1, b2)


def solution(mesh):
    in_specs = (
        P("pair", None, None),
        P(),
        P("pair", None, "trow"),
        P("pair"),
        P(),
        P(),
        P(),
        P(),
        P(),
        P(),
    )
    out_specs = P("pair", None, "trow")
    return jax.shard_map(per_device, mesh=mesh, in_specs=in_specs, out_specs=out_specs, check_vma=False)
```

time: 181 us -> 31.2 us (0.17)
  waiting for transfers between devices: 96.2 us -> 3.95 us
  other arithmetic: 19.7 us -> 0.16 us
  between operations: 15.7 us -> 2.09 us
  local copies, waits for them, and re-layouts: 19 us -> 5.51 us
  Pallas kernels: 0 us -> 9.73 us
  starting transfers between devices: 14.8 us -> 9.19 us
  blocking collectives: 4.94 us -> 0 us
  loops' own time: 4.64 us -> 0 us
  matrix products: 4.31 us -> 0 us
    psum x1 -> x0, waiting for transfers between devices: 79.5 us -> none  [broadcast(): return lax.psum(jnp.where(mine, shard, jnp.zeros_like(shard)), axis)]
    ppermute x6 -> x7, waiting for transfers between devices: 16.7 us -> 3.95 us  [swapped(): return lax.ppermute(values, axis, [(i, i ^ distance) for i in range(count)])]
    pallas_call x0 -> x2, Pallas kernels: none -> 9.73 us  [the longest x1 8.06 us: per_device(): pl.pallas_call(functools.partial(score_kernel, rows_here, n1, n2), out_sh...]
    select_n x20 -> x1, other arithmetic: 5.2 us -> 0.02 us  [spread(): held = jnp.where(rank == owner, window, jnp.zeros_like(window))]
    dynamic_update_slice x4 -> x0, other arithmetic: 4.99 us -> none  [conv_layer(): lax.map(one_block, jnp.arange(rows_out // block_rows, dtype=jnp.int32))]
    pmax x1 -> x0, blocking collectives: 4.94 us -> none  [score_pair(): peak_target = lax.pmax(jnp.max(magnitude, axis=1), 'trow')]
    another operation x3 -> x0, loops' own time: 4.64 us -> none  [conv_layer(): lax.map(one_block, jnp.arange(rows_out // block_rows, dtype=jnp.int32))]
    while x36 -> x0, local copies, waits for them, and re-layouts: 4.33 us -> none
  transfers between devices with their start and end apart: 8 -> 7, of which waited for: 6 -> 2; matrix products, arithmetic and copies ran while one was open for 5% -> 11% of each run, Pallas kernels for 0% -> 5%
where the time goes in v1:
time: 31.2 us; the launch traced here: 30.6 us
  Pallas kernels  9.73 us (31%)
  starting transfers between devices  9.19 us (29%)
  local copies, waits for them, and re-layouts  5.51 us (18%)
  waiting for transfers between devices  3.95 us (13%)
  between operations  2.09 us (7%)
    ppermute x7, starting transfers between devices, swapped(): return lax.ppermute(values, axis, [(i, i ^ distance) for i in range(count)])  9.19 us
    pallas_call x1, Pallas kernels, per_device(): pl.pallas_call(functools.partial(score_kernel, rows_here, n1, n2), out_sh...  8.06 us
    ppermute x7, waiting for transfers between devices, swapped(): return lax.ppermute(values, axis, [(i, i ^ distance) for i in range(count)])  3.95 us
    unnamed x6, local copies, waits for them, and re-layouts  2.38 us
    pallas_call x1, Pallas kernels, per_device(): pl.pallas_call(functools.partial(expand_kernel, ch), out_shape=(jax.Shape...  1.67 us
    reshape x2, local copies, waits for them, and re-layouts, per_device(): w_first.reshape(ch, 81)  0.85 us
    reshape x1, local copies, waits for them, and re-layouts, per_device(): jnp.transpose(w_last[0], (1, 2, 3, 4, 0)).reshape(81, ch)  0.78 us
    another operation x2, local copies, waits for them, and re-layouts, per_device(): b2 = jnp.tile(b_middle, lanes // ch)[None]  0.75 us
  transfers between devices with their start and end apart: 7, of which 2 were waited for; matrix products, arithmetic and copies ran while one was open for 11% of the time, Pallas kernels for 5%

profile of v1, /device:TPU:0, one launch (start us, length us, event | category | flops | bytes accessed | tf_op | source)
XLA Modules:
  0.0 30.6 jit_solution(8379621798777260638)
XLA Ops:
  0.0 0.0 copy-start.1
  0.8 0.5 %collective-permute-start.1 = (bf16[32,1024]{1,0:T(8,128)(2,1)S(1)}, bf16[32,1024]{1,0:T(8,128)(2,1)S(1)}, u32[]{:S(2)}, u32[]{:S(2)}) collective-permute-start(bf16[32,1024]{1,0:T(8,128)(2,1)S(1)} %dynamic-slice_bitcast_fusion), channel_id=1, source_target_pairs={{0,2},{2,0},{4,6},{6,4},{8,10},{10,8},{12,14},{14,12},{16,18},{18,... | collective-permute-start | bytes 196616 | tf_op jit(solution)/shard_map/ppermute | solution.py:26
  1.3 2.6 %collective-permute-start = (bf16[512,512]{1,0:T(8,128)(2,1)}, bf16[512,512]{1,0:T(8,128)(2,1)S(1)}, u32[]{:S(2)}, u32[]{:S(2)}) collective-permute-start(bf16[512,512]{1,0:T(8,128)(2,1)} %bitcast.17), channel_id=1, source_target_pairs={{0,1},{1,0},{2,3},{3,2},{4,5},{5,4},{6,7},{7,6},{8,9},{9,8},{10,11... | collective-permute-start | bytes 1572872 | tf_op jit(solution)/shard_map/ppermute | solution.py:26
  3.9 0.0 collective-permute-done.1
  3.9 1.6 %collective-permute-start.2 = (bf16[32,1024]{1,0:T(8,128)(2,1)S(1)}, bf16[32,1024]{1,0:T(8,128)(2,1)S(1)}, u32[]{:S(2)}, u32[]{:S(2)}) collective-permute-start(bf16[32,1024]{1,0:T(8,128)(2,1)S(1)} %bitcast_add_fusion), channel_id=1, source_target_pairs={{0,4},{2,6},{4,0},{6,2},{8,12},{10,14},{12,8},{14,10},{16,20},{18,... | collective-permute-start | bytes 196616 | tf_op jit(solution)/shard_map/ppermute | solution.py:26
  5.5 2.8 %collective-permute-done.2 = bf16[32,1024]{1,0:T(8,128)(2,1)S(1)} collective-permute-done((bf16[32,1024]{1,0:T(8,128)(2,1)S(1)}, bf16[32,1024]{1,0:T(8,128)(2,1)S(1)}, u32[]{:S(2)}, u32[]{:S(2)}) %collective-permute-start.2) | collective-permute-done | bytes 65568 | tf_op jit(solution)/shard_map/ppermute | solution.py:26
  8.3 3.7 %collective-permute-start.5 = (bf16[32,1024]{1,0:T(8,128)(2,1)S(1)}, bf16[32,1024]{1,0:T(8,128)(2,1)S(1)}, u32[]{:S(2)}, u32[]{:S(2)}) collective-permute-start(bf16[32,1024]{1,0:T(8,128)(2,1)S(1)} %add.30), channel_id=1, source_target_pairs={{0,24},{2,26},{4,28},{6,30},{8,16},{10,18},{12,20},{14,22},{16,8},... | collective-permute-start | bytes 196616 | tf_op jit(solution)/shard_map/ppermute | solution.py:26
  11.9 0.3 %collective-permute-start.4 = (bf16[32,1024]{1,0:T(8,128)(2,1)S(1)}, bf16[32,1024]{1,0:T(8,128)(2,1)S(1)}, u32[]{:S(2)}, u32[]{:S(2)}) collective-permute-start(bf16[32,1024]{1,0:T(8,128)(2,1)S(1)} %add.30), channel_id=1, source_target_pairs={{0,16},{2,18},{4,20},{6,22},{8,24},{10,26},{12,28},{14,30},{16,0},... | collective-permute-start | bytes 196616 | tf_op jit(solution)/shard_map/ppermute | solution.py:26
  12.3 0.5 %collective-permute-start.3 = (bf16[32,1024]{1,0:T(8,128)(2,1)S(1)}, bf16[32,1024]{1,0:T(8,128)(2,1)S(1)}, u32[]{:S(2)}, u32[]{:S(2)}) collective-permute-start(bf16[32,1024]{1,0:T(8,128)(2,1)S(1)} %add.30), channel_id=1, source_target_pairs={{0,8},{2,10},{4,12},{6,14},{8,0},{10,2},{12,4},{14,6},{16,24},{18,... | collective-permute-start | bytes 196616 | tf_op jit(solution)/shard_map/ppermute | solution.py:26
  14.0 0.8 %reshape.16 = bf16[16,81]{0,1:T(8,128)(2,1)S(1)} reshape(bf16[16,1,3,3,3,3]{0,5,4,3,2,1:T(4,128)(2,1)} %param.14) | data formatting | bytes 5184 | tf_op jit(solution)/shard_map/reshape | solution.py:293
  14.8 0.1 copy.12.wf_ref
  14.9 0.8 %reshape.18.wl_ref = bf16[81,16]{1,0:T(8,128)(2,1)S(1)} reshape(bf16[3,3,3,3,16]{4,3,2,1,0:T(4,128)(2,1)} %bitcast.20) | data formatting | bytes 5184 | tf_op jit(solution)/shard_map/reshape | solution.py:295
  15.6 0.7 %tile.4 = f32[64,16]{1,0:T(8,128)S(1)} broadcast(f32[16]{0:T(128)} %param.15), dimensions={1} | broadcast | bytes 4160 | tf_op jit(solution)/shard_map/tile | solution.py:297
  16.3 0.1 broadcast_in_dim_tile.6.b1_ref
  16.4 0.7 %tile.5 = f32[64,16]{1,0:T(8,128)S(1)} broadcast(f32[16]{0:T(128)} %param.17), dimensions={1} | broadcast | bytes 4160 | tf_op jit(solution)/shard_map/tile | solution.py:298
  17.1 0.1 broadcast_in_dim_tile.7.b2_ref
  17.1 0.0 copy-start.2
  17.1 1.0 %copy-done.2 = bf16[16,16,3,3,3,3]{1,0,5,4,3,2:T(8,128)(2,1)S(1)} copy-done((bf16[16,16,3,3,3,3]{1,0,5,4,3,2:T(8,128)(2,1)S(1)}, bf16[16,16,3,3,3,3]{1,0,5,4,3,2:T(8,128)(2,1)}, u32[]{:S(2)}) %copy-start.2) | copy-done | bytes 41496
  18.1 1.7 %expand.1 = (bf16[3,1024,256]{2,1,0:T(8,128)(2,1)S(1)}, bf16[9,256,512]{2,1,0:T(8,128)(2,1)S(1)}, bf16[3,256,1024]{2,1,0:T(8,128)(2,1)S(1)}) custom-call(bf16[16,81]{1,0:T(8,128)(2,1)S(1)} %copy.12.wf_ref, bf16[81,16,16]{2,1,0:T(8,128)(2,1)S(1)} %bitcast.19, bf16[81,16]{1,0:T(8,128)(2,1)S(1)} %reshape.18.wl_ref), custom_call_target="tpu_custom_call" | custom-call | tf_op jit(solution)/shard_map/expand/pallas_call | solution.py:281
  19.8 0.0 copy-start
  19.8 1.4 %copy-done = bf16[9,256,512]{2,1,0:T(8,128)(2,1)} copy-done((bf16[9,256,512]{2,1,0:T(8,128)(2,1)}, bf16[9,256,512]{2,1,0:T(8,128)(2,1)S(1)}, u32[]{:S(2)}) %copy-start) | copy-done | bytes 2359320
  21.2 0.0 collective-permute-done.5
  21.2 0.0 collective-permute-done.4
  21.2 0.0 collective-permute-done.3
  21.2 0.1 collective-permute-start.6
  21.3 0.1 pad_add_fusion.s_ref
  21.4 1.2 %collective-permute-done.6.qb_ref = bf16[32,1024]{1,0:T(8,128)(2,1)S(1)} collective-permute-done((bf16[32,1024]{1,0:T(8,128)(2,1)S(1)}, bf16[32,1024]{1,0:T(8,128)(2,1)S(1)}, u32[]{:S(2)}, u32[]{:S(2)}) %collective-permute-start.6) | collective-permute-done | bytes 65568 | tf_op jit(solution)/shard_map/ppermute | solution.py:26
  22.6 0.0 collective-permute-done.to_ref
  22.6 0.0 copy-done.1
  22.6 8.1 %score.1 = f32[1,64,256]{2,1,0:T(8,128)} custom-call(s32[3]{0:T(128)S(1)} %pad_add_fusion.s_ref, f32[1]{0:T(128)S(6)} %copy.15.b3_ref, bf16[512,512]{1,0:T(8,128)(2,1)S(1)} %bitcast.18, bf16[512,512]{1,0:T(8,128)(2,1)S(1)} %collective-permute-done.to_ref, bf16[32,1024]{1,0:T(8,128)(2,1)S(1)} %add_add_fusion.qa_ref, ...), custom_call_target="tpu_custom_call" | custom-call | tf_op jit(solution)/shard_map/score/pallas_call | solution.py:300
  (5 shorter events, 0.1 us)
Async XLA Ops:
  0.0 22.6 %copy-start.1 = (bf16[1,512,512]{2,1,0:T(8,128)(2,1)S(1)}, bf16[1,512,512]{2,1,0:T(8,128)(2,1)}, u32[]{:S(2)}) copy-start(bf16[1,512,512]{2,1,0:T(8,128)(2,1)} %param.12) | copy-start | bytes 1572868
  0.8 3.1 %collective-permute-start.1 = (bf16[32,1024]{1,0:T(8,128)(2,1)S(1)}, bf16[32,1024]{1,0:T(8,128)(2,1)S(1)}, u32[]{:S(2)}, u32[]{:S(2)}) collective-permute-start(bf16[32,1024]{1,0:T(8,128)(2,1)S(1)} %dynamic-slice_bitcast_fusion), channel_id=1, source_target_pairs={{0,2},{2,0},{4,6},{6,4},{8,10},{10,8},{12,14},{14,12},{16,18},{18,... | collective-permute-start | bytes 196616 | tf_op jit(solution)/shard_map/ppermute | solution.py:26
  1.3 21.3 %collective-permute-start = (bf16[512,512]{1,0:T(8,128)(2,1)}, bf16[512,512]{1,0:T(8,128)(2,1)S(1)}, u32[]{:S(2)}, u32[]{:S(2)}) collective-permute-start(bf16[512,512]{1,0:T(8,128)(2,1)} %bitcast.17), channel_id=1, source_target_pairs={{0,1},{1,0},{2,3},{3,2},{4,5},{5,4},{6,7},{7,6},{8,9},{9,8},{10,11... | collective-permute-start | bytes 1572872 | tf_op jit(solution)/shard_map/ppermute | solution.py:26
  3.9 4.3 %collective-permute-start.2 = (bf16[32,1024]{1,0:T(8,128)(2,1)S(1)}, bf16[32,1024]{1,0:T(8,128)(2,1)S(1)}, u32[]{:S(2)}, u32[]{:S(2)}) collective-permute-start(bf16[32,1024]{1,0:T(8,128)(2,1)S(1)} %bitcast_add_fusion), channel_id=1, source_target_pairs={{0,4},{2,6},{4,0},{6,2},{8,12},{10,14},{12,8},{14,10},{16,20},{18,... | collective-permute-start | bytes 196616 | tf_op jit(solution)/shard_map/ppermute | solution.py:26
  8.3 12.9 %collective-permute-start.5 = (bf16[32,1024]{1,0:T(8,128)(2,1)S(1)}, bf16[32,1024]{1,0:T(8,128)(2,1)S(1)}, u32[]{:S(2)}, u32[]{:S(2)}) collective-permute-start(bf16[32,1024]{1,0:T(8,128)(2,1)S(1)} %add.30), channel_id=1, source_target_pairs={{0,24},{2,26},{4,28},{6,30},{8,16},{10,18},{12,20},{14,22},{16,8},... | collective-permute-start | bytes 196616 | tf_op jit(solution)/shard_map/ppermute | solution.py:26
  11.9 9.3 %collective-permute-start.4 = (bf16[32,1024]{1,0:T(8,128)(2,1)S(1)}, bf16[32,1024]{1,0:T(8,128)(2,1)S(1)}, u32[]{:S(2)}, u32[]{:S(2)}) collective-permute-start(bf16[32,1024]{1,0:T(8,128)(2,1)S(1)} %add.30), channel_id=1, source_target_pairs={{0,16},{2,18},{4,20},{6,22},{8,24},{10,26},{12,28},{14,30},{16,0},... | collective-permute-start | bytes 196616 | tf_op jit(solution)/shard_map/ppermute | solution.py:26
  12.3 9.0 %collective-permute-start.3 = (bf16[32,1024]{1,0:T(8,128)(2,1)S(1)}, bf16[32,1024]{1,0:T(8,128)(2,1)S(1)}, u32[]{:S(2)}, u32[]{:S(2)}) collective-permute-start(bf16[32,1024]{1,0:T(8,128)(2,1)S(1)} %add.30), channel_id=1, source_target_pairs={{0,8},{2,10},{4,12},{6,14},{8,0},{10,2},{12,4},{14,6},{16,24},{18,... | collective-permute-start | bytes 196616 | tf_op jit(solution)/shard_map/ppermute | solution.py:26
  17.1 1.0 %copy-start.2 = (bf16[16,16,3,3,3,3]{1,0,5,4,3,2:T(8,128)(2,1)S(1)}, bf16[16,16,3,3,3,3]{1,0,5,4,3,2:T(8,128)(2,1)}, u32[]{:S(2)}) copy-start(bf16[16,16,3,3,3,3]{1,0,5,4,3,2:T(8,128)(2,1)} %param.16) | copy-start | bytes 124420
  19.8 1.4 %copy-start = (bf16[9,256,512]{2,1,0:T(8,128)(2,1)}, bf16[9,256,512]{2,1,0:T(8,128)(2,1)S(1)}, u32[]{:S(2)}) copy-start(bf16[9,256,512]{2,1,0:T(8,128)(2,1)S(1)} %get-tuple-element.9.w2_ref) | copy-start | bytes 7077892
  21.2 1.3 %collective-permute-start.6 = (bf16[32,1024]{1,0:T(8,128)(2,1)S(1)}, bf16[32,1024]{1,0:T(8,128)(2,1)S(1)}, u32[]{:S(2)}, u32[]{:S(2)}) collective-permute-start(bf16[32,1024]{1,0:T(8,128)(2,1)S(1)} %add_add_fusion.qa_ref), channel_id=1, source_target_pairs={{0,2},{2,0},{4,6},{6,4},{8,10},{10,8},{12,14},{14,12},{16,18},{18,... | collective-permute-start | bytes 196616 | tf_op jit(solution)/shard_map/ppermute | solution.py:26

commit v2 on v1

--- a/solution.py
+++ b/solution.py
@@ -18,7 +18,10 @@
 BF16 = jnp.bfloat16
 NT = (((1,), (1,)), ((), ()))
 PITCH = WB + 8
-VMEM_LIMIT = 48 * 1024 * 1024
+VMEM_LIMIT = 16 * 1024 * 1024
+VMEM = pl.BlockSpec(memory_space=pltpu.VMEM)
+SMEM = pl.BlockSpec(memory_space=pltpu.SMEM)
+HBM = pl.BlockSpec(memory_space=pltpu.HBM)
 
 
 def swapped(values, axis, distance):
@@ -26,15 +29,34 @@
     return lax.ppermute(values, axis, [(i, i ^ distance) for i in range(count)])
 
 
+def front_kernel(rank_ref, window_hbm, keep_ref, give_ref, sems):
+    half = keep_ref.shape[0]
+    bit = rank_ref[0] % 2
+    copies = [
+        pltpu.make_async_copy(window_hbm.at[pl.ds(pl.multiple_of(which * half, half), half)], ref, sems.at[n])
+        for n, (which, ref) in enumerate(((bit, keep_ref), (1 - bit, give_ref)))
+    ]
+    for copy in copies:
+        copy.start()
+    for copy in copies:
+        copy.wait()
+
+
 def spread(window, owner, axis):
     count = lax.axis_size(axis)
     rank = lax.axis_index(axis)
-    held = jnp.where(rank == owner, window, jnp.zeros_like(window))
-    half = window.shape[0] // 2
-    bit = rank % 2
-    keep = lax.dynamic_slice_in_dim(held, bit * half, half, 0)
-    give = lax.dynamic_slice_in_dim(held, (1 - bit) * half, half, 0)
-    held = keep + swapped(give, axis, 1)
+    half = jax.ShapeDtypeStruct((window.shape[0] // 2, window.shape[1]), window.dtype)
+    keep, give = pl.pallas_call(
+        front_kernel,
+        out_shape=(half, half),
+        in_specs=[SMEM, HBM],
+        out_specs=(VMEM, VMEM),
+        scratch_shapes=[pltpu.SemaphoreType.DMA((2,))],
+        compiler_params=pltpu.CompilerParams(vmem_limit_bytes=VMEM_LIMIT),
+        name="front",
+    )(rank.reshape(1), in_hbm(window))
+    held = jnp.where(rank == owner, keep, swapped(give, axis, 1))
+    held = jnp.where(rank // 2 == owner // 2, held, jnp.zeros_like(held))
     bits = [1 << b for b in range(1, count.bit_length() - 1)]
     rounds = []
     if len(bits) % 2:
@@ -48,6 +70,10 @@
     return held, swapped(held, axis, 1)
 
 
+def in_hbm(array):
+    return pltpu.with_memory_space_constraint(array, pltpu.HBM)
+
+
 def dot(left, right):
     return jnp.dot(left, right, preferred_element_type=F32)
 
@@ -64,18 +90,47 @@
     return jnp.where(cond, 1.0, 0.0).astype(BF16)
 
 
-def expand_kernel(ch, wf_ref, wm_ref, wl_ref, w1_ref, w2_ref, w3_ref):
+def expand_kernel(
+    ch, misc_ref, wf_hbm, wm_hbm, wl_hbm, w1_ref, w2_ref, w3_ref, rows_ref, wf_ref, wm_ref, wl_ref, sems
+):
     group = 2 * ch
-    index = lambda i, j, k, l: ((i * 3 + j) * 3 + k) * 3 + l
-
-    taps = wf_ref[...]
-    lane = iota((81, 128), 1)
-    src = iota((81, 128), 0)
+    pairs = ((wf_hbm, wf_ref), (wm_hbm, wm_ref), (wl_hbm, wl_ref))
+    copies = [pltpu.make_async_copy(src, dst, sems.at[n]) for n, (src, dst) in enumerate(pairs)]
+    for copy in copies:
+        copy.start()
+
+    misc = misc_ref[...]
+    chan = iota((8, 128), 1)
+    for n in range(2):
+        total = jnp.where(chan < ch, pltpu.roll(misc, 128 - n * ch, 1) if n else misc, 0.0)
+        size = ch
+        while size < 128:
+            total = total + pltpu.roll(total, size, 1)
+            size *= 2
+        rows_ref[n : n + 1, 0:128] = total[0:1]
+        rows_ref[n : n + 1, 128:256] = total[0:1]
+    for n in range(2):
+        at = 2 * ch + n
+        rows_ref[2 + n : 3 + n, :] = jnp.broadcast_to(misc[0:1, at : at + 1], (1, 256))
+
+    for copy in copies:
+        copy.wait()
+
+    def by_offset(ref):
+        values = ref[...].astype(F32)
+        fill = jnp.zeros((32 - values.shape[0], ch), F32)
+        return jnp.concatenate([part for l in range(3) for part in (values[:, l, :], fill)], axis=0)
+
+    taps = by_offset(wf_ref)
+    taps = jnp.concatenate([taps, jnp.zeros((32, ch), F32)], axis=0)
+    taps = jnp.concatenate([taps, jnp.zeros((128, 128 - ch), F32)], axis=1).T[:ch].astype(BF16)
+    lane = iota((128, 128), 1)
+    src = iota((128, 128), 0)
     base = []
     for k in range(3):
         for ra in range(2):
             l, rp, j = lane // 6, (lane // 3) % 2, lane % 3
-            want = (((rp - ra + 1) * 3 + j) * 3 + k) * 3 + l
+            want = l * 32 + ((rp - ra + 1) * 3 + j) * 3 + k
             base.append(dot(taps, one_hot((src == want) & (lane < 18))))
     base = jnp.concatenate(base, axis=0).astype(BF16)
     row = iota((128, 256), 0)
@@ -94,7 +149,7 @@
     for j in range(3):
         for rp in range(2):
             picked = jnp.concatenate(
-                [wm_ref[index(rp - ra + 1, j, k, l)] for k in range(3) for l in range(3) for ra in range(2)],
+                [wm_ref[(((rp - ra + 1) * 3 + j) * 3 + k) * 3 + l] for k in range(3) for l in range(3) for ra in range(2)],
                 axis=0,
             )
             part = dot(picked, one_hot(col == j * group + rp * ch + row))
@@ -113,16 +168,16 @@
                 chunk = piece[:, :128] if v == a else piece[:, 128:] if v == a + 1 else blank
                 w2_ref[tap, ca * group : (ca + 1) * group, v * 128 : (v + 1) * 128] = chunk
 
-    taps = wl_ref[...]
-    out_row = iota((24, 81), 0)
-    src = iota((24, 81), 1)
+    taps = by_offset(wl_ref).astype(BF16)
+    out_row = iota((24, 96), 0)
+    src = iota((24, 96), 1)
     row = iota((ch, 128), 0)
     col = iota((ch, 128), 1)
     total = None
     for j in range(3):
         for rp in range(2):
             k, l, ra = out_row // 8, (out_row % 8) // 2, out_row % 2
-            want = (((rp - ra + 1) * 3 + j) * 3 + k) * 3 + l
+            want = l * 32 + ((rp - ra + 1) * 3 + j) * 3 + k
             picked = dot(one_hot((src == want) & (l < 3)), taps).astype(BF16)
             part = dot(picked, one_hot(col == j * group + rp * ch + row))
             total = part if total is None else total + part
@@ -144,10 +199,11 @@
 
 
 def score_kernel(
-    rows_here, n1, n2, s_ref, b3_ref, tm_ref, to_ref, qa_ref, qb_ref, w1_ref, w2_ref, w3_ref, b1_ref, b2_ref,
+    rows_here, n1, n2, s_ref, rows_ref, tm_ref, to_ref, qa_ref, qb_ref, w1_ref, w2_ref, w3_ref,
     out_ref, v_ref, x_ref, h1_ref, h2_ref, ya_ref, yb_ref, yt_ref,
 ):
-    count, trow, bit = s_ref[0], s_ref[1], s_ref[2]
+    trow, bit = s_ref[0], s_ref[1]
+    count = rows_ref[3:4, :]
     cells = tm_ref.shape[0]
     grid_rows = cells // WB
     width = tm_ref.shape[1]
@@ -174,7 +230,7 @@
         return jnp.sum(values * values, axis=1, keepdims=True)
 
     inv = lax.rsqrt(squares(tm_ref) + squares(to_ref) + EPS_NORM)
-    live = iota((cells, 128), 0) // WB < count
+    live = (iota((cells, 128), 0) // WB).astype(F32) < count[:, :128]
     corr = jnp.where(live, scale * raw * inv, 0.0)
     mag = jnp.abs(corr)
     peak_query = jnp.max(mag, axis=1, keepdims=True)
@@ -204,9 +260,10 @@
     h2_ref[0] = zero[:WB]
     h2_ref[n2 + 1] = zero[:WB]
     step = iota((n1 * half, 256), 0) % half
+    bias1, bias2 = rows_ref[0:1, :], rows_ref[1:2, :]
     for q in range(lanes // 256):
         cols = slice(q * 256, (q + 1) * 256)
-        total = b1_ref[:, cols]
+        total = bias1
         for k in range(3):
             total = total + dot_nt(x_ref[k : k + n1].reshape(n1 * WB, 256), w1_ref[k, cols, :])
         total = jnp.maximum(total, 0.0)
@@ -223,7 +280,7 @@
     for q in range(lanes // 256):
         cols = slice(q * 256, (q + 1) * 256)
         lo, hi = max(q * 256 - 128, 0), min(q * 256 + 384, lanes)
-        total = b2_ref[:, cols]
+        total = bias2
         for k in range(3):
             for l in range(3):
                 cells_in = h1_ref[pl.ds(off2 + k, n2), l * half : l * half + WB, lo:hi].reshape(n2 * WB, hi - lo)
@@ -245,7 +302,7 @@
         yt_ref[v, 0:128, :] = ya_ref[v * 128 : (v + 1) * 128, :].T
         yt_ref[v, 128:256, :] = yb_ref[v * 128 : (v + 1) * 128, :].T
     lane = iota((WA, here), 1)
-    keep = rows_here * trow + lane // WB < count
+    keep = (rows_here * trow + lane // WB).astype(F32) < count[:, :1]
     for ra in range(2):
         parts = [
             jnp.concatenate([yt_ref[v, pl.ds(l * 2 + ra, WA, stride=8), :] for v in range(here // 128)], axis=1)
@@ -253,7 +310,7 @@
         ]
         before = jnp.where(lane % WB == 0, 0.0, pltpu.roll(parts[0], 1, 1))
         after = jnp.where(lane % WB == WB - 1, 0.0, pltpu.roll(parts[2], here - 1, 1))
-        result = before + parts[1] + after + b3_ref[0]
+        result = before + parts[1] + after + rows_ref[2:3, :1]
         out_ref[0, ra * WA : (ra + 1) * WA, :] = jnp.where(keep, result, 0.0)
 
 
@@ -274,34 +331,39 @@
 
     other = swapped(target, "trow", 1)
     own, sibling = spread(query_bank[0], ref_owner[0], "pair")
-    scalars = jnp.stack([valid_rows[0], lax.axis_index("trow"), lax.axis_index("pair") % 2]).astype(jnp.int32)
-
-    vmem = pl.BlockSpec(memory_space=pltpu.VMEM)
-    smem = pl.BlockSpec(memory_space=pltpu.SMEM)
-    w1, w2, w3 = pl.pallas_call(
+    ranks = jnp.stack([lax.axis_index("trow"), lax.axis_index("pair") % 2]).astype(jnp.int32)
+
+    misc = jnp.concatenate([b_first, b_middle, b_last, valid_rows.astype(F32)])
+    w1, w2, w3, rows = pl.pallas_call(
         functools.partial(expand_kernel, ch),
         out_shape=(
             jax.ShapeDtypeStruct((3, lanes, 256), BF16),
             jax.ShapeDtypeStruct((9, 256, 512), BF16),
             jax.ShapeDtypeStruct((3, 256, lanes), BF16),
+            jax.ShapeDtypeStruct((8, 256), F32),
         ),
-        in_specs=[vmem] * 3,
-        out_specs=(vmem,) * 3,
+        in_specs=[VMEM] + [HBM] * 3,
+        out_specs=(VMEM,) * 4,
+        scratch_shapes=[
+            pltpu.VMEM((27, 3, ch), BF16),
+            pltpu.VMEM((81, ch, ch), BF16),
+            pltpu.VMEM((27, 3, ch), BF16),
+            pltpu.SemaphoreType.DMA((3,)),
+        ],
         compiler_params=pltpu.CompilerParams(vmem_limit_bytes=VMEM_LIMIT),
         name="expand",
     )(
-        w_first.reshape(ch, 81),
-        jnp.transpose(w_middle, (2, 3, 4, 5, 0, 1)).reshape(81, ch, ch),
-        jnp.transpose(w_last[0], (1, 2, 3, 4, 0)).reshape(81, ch),
+        jnp.broadcast_to(jnp.pad(misc, (0, 128 - misc.shape[0])), (8, 128)),
+        in_hbm(jnp.transpose(w_first, (1, 2, 3, 4, 5, 0)).reshape(27, 3, ch)),
+        in_hbm(jnp.transpose(w_middle, (2, 3, 4, 5, 0, 1)).reshape(81, ch, ch)),
+        in_hbm(jnp.transpose(w_last, (0, 2, 3, 4, 5, 1)).reshape(27, 3, ch)),
     )
-    b1 = jnp.tile(b_first, lanes // ch)[None]
-    b2 = jnp.tile(b_middle, lanes // ch)[None]
 
     return pl.pallas_call(
         functools.partial(score_kernel, rows_here, n1, n2),
         out_shape=jax.ShapeDtypeStruct((1, positions, rows_here * WB), F32),
-        in_specs=[smem, smem] + [vmem] * 9,
-        out_specs=vmem,
+        in_specs=[SMEM] + [VMEM] * 8,
+        out_specs=VMEM,
         scratch_shapes=[
             pltpu.VMEM((8 + (grid_rows + 2) * PITCH, 128), F32),
             pltpu.VMEM((n1 + 2, WB, 256), BF16),
@@ -313,7 +375,7 @@
         ],
         compiler_params=pltpu.CompilerParams(vmem_limit_bytes=VMEM_LIMIT),
         name="score",
-    )(scalars, b_last, target, other, own, sibling, w1, w2, w3, b1, b2)
+    )(ranks, rows, target, other, own, sibling, w1, w2, w3)
 
 
 def solution(mesh):

time: 31.2 us -> 26.5 us (0.85); the launches traced: 30.6 us -> 26.3 us
  local copies, waits for them, and re-layouts: 5.51 us -> 0.01 us
  Pallas kernels: 9.73 us -> 10.7 us
  other arithmetic: 0.16 us -> 0.88 us
  waiting for transfers between devices: 3.95 us -> 3.55 us
    unnamed x6 -> x2, local copies, waits for them, and re-layouts: 2.38 us -> 0.01 us
    reshape x3 -> x0, local copies, waits for them, and re-layouts: 1.63 us -> none  [the longest x2 0.85 us: per_device(): w_first.reshape(ch, 81)]
    another operation x4 -> x0, local copies, waits for them, and re-layouts: 1.49 us -> none  [the longest x2 0.75 us: per_device(): b2 = jnp.tile(b_middle, lanes // ch)[None]]
    pallas_call x1, Pallas kernels: 8.06 us -> 6.88 us  [per_device(): pl.pallas_call(functools.partial(score_kernel, rows_here, n1, n2), out_sh...]
    pallas_call x1, Pallas kernels: 1.67 us -> 2.84 us  [per_device(): pl.pallas_call(functools.partial(expand_kernel, ch), out_shape=(jax.Shape...]
    pallas_call x0 -> x1, Pallas kernels: none -> 0.95 us  [spread(): pl.pallas_call(front_kernel, out_shape=(half, half), in_specs=[SMEM, HBM]...]
    concatenate x0 -> x1, other arithmetic: none -> 0.75 us  [per_device(): misc = jnp.concatenate([b_first, b_middle, b_last, valid_rows.astype(F32)])]
    ppermute x7, waiting for transfers between devices: 3.95 us -> 3.55 us  [swapped(): return lax.ppermute(values, axis, [(i, i ^ distance) for i in range(count)])]
  transfers between devices with their start and end apart: 7 -> 7, of which waited for: 2 -> 3; matrix products, arithmetic and copies ran while one was open for 11% -> 3% of each run, Pallas kernels for 5% -> 11%
where the time goes in v2:
time: 26.5 us; the launch traced here: 26.3 us
  Pallas kernels  10.7 us (40%)
  starting transfers between devices  9.19 us (35%)
  waiting for transfers between devices  3.55 us (13%)
  between operations  2.04 us (8%)
  other arithmetic  0.88 us (3%)
    ppermute x7, starting transfers between devices, swapped(): return lax.ppermute(values, axis, [(i, i ^ distance) for i in range(count)])  9.19 us
    pallas_call x1, Pallas kernels, per_device(): pl.pallas_call(functools.partial(score_kernel, rows_here, n1, n2), out_sh...  6.88 us
    ppermute x7, waiting for transfers between devices, swapped(): return lax.ppermute(values, axis, [(i, i ^ distance) for i in range(count)])  3.55 us
    pallas_call x1, Pallas kernels, per_device(): pl.pallas_call(functools.partial(expand_kernel, ch), out_shape=(jax.Shape...  2.84 us
    pallas_call x1, Pallas kernels, spread(): pl.pallas_call(front_kernel, out_shape=(half, half), in_specs=[SMEM, HBM]...  0.95 us
    concatenate x1, other arithmetic, per_device(): misc = jnp.concatenate([b_first, b_middle, b_last, valid_rows.astype(F32)])  0.75 us
  transfers between devices with their start and end apart: 7, of which 3 were waited for; matrix products, arithmetic and copies ran while one was open for 3% of the time, Pallas kernels for 11%

profile of v2, /device:TPU:0, one launch (start us, length us, event | category | flops | bytes accessed | tf_op | source)
XLA Modules:
  0.0 26.3 jit_solution(7925227185546353097)
XLA Ops:
  0.0 0.0 copy-start
  0.0 0.9 %front.1 = (bf16[32,1024]{1,0:T(8,128)(2,1)S(1)}, bf16[32,1024]{1,0:T(8,128)(2,1)S(1)}) custom-call(s32[1]{0:T(128)} %bitcast.10.rank_ref, bf16[64,1024]{1,0:T(8,128)(2,1)} %bitcast.23), custom_call_target="tpu_custom_call" | custom-call | tf_op jit(solution)/shard_map/front/pallas_call | solution.py:49
  1.0 0.5 %collective-permute-start.1 = (bf16[32,1024]{1,0:T(8,128)(2,1)S(1)}, bf16[32,1024]{1,0:T(8,128)(2,1)S(1)}, u32[]{:S(2)}, u32[]{:S(2)}) collective-permute-start(bf16[32,1024]{1,0:T(8,128)(2,1)S(1)} %get-tuple-element.13), channel_id=1, source_target_pairs={{0,2},{2,0},{4,6},{6,4},{8,10},{10,8},{12,14},{14,12},{16,18},{18,... | collective-permute-start | bytes 196616 | tf_op jit(solution)/shard_map/ppermute | solution.py:29
  1.5 2.6 %collective-permute-start = (bf16[512,512]{1,0:T(8,128)(2,1)}, bf16[512,512]{1,0:T(8,128)(2,1)S(1)}, u32[]{:S(2)}, u32[]{:S(2)}) collective-permute-start(bf16[512,512]{1,0:T(8,128)(2,1)} %bitcast.20), channel_id=1, source_target_pairs={{0,1},{1,0},{2,3},{3,2},{4,5},{5,4},{6,7},{7,6},{8,9},{9,8},{10,11... | collective-permute-start | bytes 1572872 | tf_op jit(solution)/shard_map/ppermute | solution.py:29
  4.7 0.0 collective-permute-done.1
  4.8 1.6 %collective-permute-start.2 = (bf16[32,1024]{1,0:T(8,128)(2,1)S(1)}, bf16[32,1024]{1,0:T(8,128)(2,1)S(1)}, u32[]{:S(2)}, u32[]{:S(2)}) collective-permute-start(bf16[32,1024]{1,0:T(8,128)(2,1)S(1)} %select_select_fusion), channel_id=1, source_target_pairs={{0,4},{2,6},{4,0},{6,2},{8,12},{10,14},{12,8},{14,10},{16,20},{18,... | collective-permute-start | bytes 196616 | tf_op jit(solution)/shard_map/ppermute | solution.py:29
  7.6 1.5 %collective-permute-done.2 = bf16[32,1024]{1,0:T(8,128)(2,1)S(1)} collective-permute-done((bf16[32,1024]{1,0:T(8,128)(2,1)S(1)}, bf16[32,1024]{1,0:T(8,128)(2,1)S(1)}, u32[]{:S(2)}, u32[]{:S(2)}) %collective-permute-start.2) | collective-permute-done | bytes 65568 | tf_op jit(solution)/shard_map/ppermute | solution.py:29
  9.1 3.7 %collective-permute-start.5 = (bf16[32,1024]{1,0:T(8,128)(2,1)S(1)}, bf16[32,1024]{1,0:T(8,128)(2,1)S(1)}, u32[]{:S(2)}, u32[]{:S(2)}) collective-permute-start(bf16[32,1024]{1,0:T(8,128)(2,1)S(1)} %add.21), channel_id=1, source_target_pairs={{0,24},{2,26},{4,28},{6,30},{8,16},{10,18},{12,20},{14,22},{16,8},... | collective-permute-start | bytes 196616 | tf_op jit(solution)/shard_map/ppermute | solution.py:29
  12.8 0.0 collective-permute-start.4
  12.8 0.8 %collective-permute-start.3 = (bf16[32,1024]{1,0:T(8,128)(2,1)S(1)}, bf16[32,1024]{1,0:T(8,128)(2,1)S(1)}, u32[]{:S(2)}, u32[]{:S(2)}) collective-permute-start(bf16[32,1024]{1,0:T(8,128)(2,1)S(1)} %add.21), channel_id=1, source_target_pairs={{0,8},{2,10},{4,12},{6,14},{8,0},{10,2},{12,4},{14,6},{16,24},{18,... | collective-permute-start | bytes 196616 | tf_op jit(solution)/shard_map/ppermute | solution.py:29
  13.6 0.7 %select_maximum_fusion = f32[128]{0:T(128)S(1)} fusion(f32[1]{0:T(128)S(6)} %convert_element_type.5, f32[1]{0:T(128)S(6)} %copy.13, f32[16]{0:T(128)} %param.17, f32[16]{0:T(128)} %param.15), kind=kLoop, calls=%fused_computation.2 | loop fusion | flops 1024 | bytes 648 | tf_op jit(solution)/shard_map/concatenate | solution.py:336
  14.3 2.8 %expand.1 = (bf16[3,1024,256]{2,1,0:T(8,128)(2,1)S(1)}, bf16[9,256,512]{2,1,0:T(8,128)(2,1)S(1)}, bf16[3,256,1024]{2,1,0:T(8,128)(2,1)S(1)}, f32[8,256]{1,0:T(8,128)S(1)}) custom-call(f32[8,128]{1,0:T(8,128)S(1)} %broadcast_in_dim.6.misc_ref, bf16[27,3,16]{2,1,0:T(4,128)(2,1)} %bitcast.24, bf16[81,16,16]{2,1,0:T(8,128)(2,1)} %bitcast.22, ...), custom_call_target="tpu_custom_call" | custom-call | tf_op jit(solution)/shard_map/expand/pallas_call | solution.py:337
  17.2 0.0 collective-permute-done.5
  17.2 0.9 %collective-permute-done.4 = bf16[32,1024]{1,0:T(8,128)(2,1)S(1)} collective-permute-done((bf16[32,1024]{1,0:T(8,128)(2,1)S(1)}, bf16[32,1024]{1,0:T(8,128)(2,1)S(1)}, u32[]{:S(2)}, u32[]{:S(2)}) %collective-permute-start.4) | collective-permute-done | bytes 65568 | tf_op jit(solution)/shard_map/ppermute | solution.py:29
  18.1 0.0 collective-permute-done.3
  18.1 0.1 collective-permute-start.6
  18.2 0.1 pad_add_fusion.s_ref
  18.3 1.2 %collective-permute-done.6.qb_ref = bf16[32,1024]{1,0:T(8,128)(2,1)S(1)} collective-permute-done((bf16[32,1024]{1,0:T(8,128)(2,1)S(1)}, bf16[32,1024]{1,0:T(8,128)(2,1)S(1)}, u32[]{:S(2)}, u32[]{:S(2)}) %collective-permute-start.6) | collective-permute-done | bytes 65568 | tf_op jit(solution)/shard_map/ppermute | solution.py:29
  19.4 0.0 collective-permute-done.to_ref
  19.4 0.0 copy-done
  19.4 6.9 %score.1 = f32[1,64,256]{2,1,0:T(8,128)} custom-call(s32[2]{0:T(128)S(1)} %pad_add_fusion.s_ref, f32[8,256]{1,0:T(8,128)S(1)} %get-tuple-element.11.rows_ref, bf16[512,512]{1,0:T(8,128)(2,1)S(1)} %bitcast.21, bf16[512,512]{1,0:T(8,128)(2,1)S(1)} %collective-permute-done.to_ref, bf16[32,1024]{1,0:T(8,128)(2,1)S(1)} %add_add_fusion.qa_ref, ...), custom_call_target="tpu_custom_call" | custom-call | tf_op jit(solution)/shard_map/score/pallas_call | solution.py:362
  (4 shorter events, 0.1 us)
Async XLA Ops:
  0.0 19.4 %copy-start = (bf16[1,512,512]{2,1,0:T(8,128)(2,1)S(1)}, bf16[1,512,512]{2,1,0:T(8,128)(2,1)}, u32[]{:S(2)}) copy-start(bf16[1,512,512]{2,1,0:T(8,128)(2,1)} %param.12) | copy-start | bytes 1572868
  1.0 3.8 %collective-permute-start.1 = (bf16[32,1024]{1,0:T(8,128)(2,1)S(1)}, bf16[32,1024]{1,0:T(8,128)(2,1)S(1)}, u32[]{:S(2)}, u32[]{:S(2)}) collective-permute-start(bf16[32,1024]{1,0:T(8,128)(2,1)S(1)} %get-tuple-element.13), channel_id=1, source_target_pairs={{0,2},{2,0},{4,6},{6,4},{8,10},{10,8},{12,14},{14,12},{16,18},{18,... | collective-permute-start | bytes 196616 | tf_op jit(solution)/shard_map/ppermute | solution.py:29
  1.5 18.0 %collective-permute-start = (bf16[512,512]{1,0:T(8,128)(2,1)}, bf16[512,512]{1,0:T(8,128)(2,1)S(1)}, u32[]{:S(2)}, u32[]{:S(2)}) collective-permute-start(bf16[512,512]{1,0:T(8,128)(2,1)} %bitcast.20), channel_id=1, source_target_pairs={{0,1},{1,0},{2,3},{3,2},{4,5},{5,4},{6,7},{7,6},{8,9},{9,8},{10,11... | collective-permute-start | bytes 1572872 | tf_op jit(solution)/shard_map/ppermute | solution.py:29
  4.8 4.3 %collective-permute-start.2 = (bf16[32,1024]{1,0:T(8,128)(2,1)S(1)}, bf16[32,1024]{1,0:T(8,128)(2,1)S(1)}, u32[]{:S(2)}, u32[]{:S(2)}) collective-permute-start(bf16[32,1024]{1,0:T(8,128)(2,1)S(1)} %select_select_fusion), channel_id=1, source_target_pairs={{0,4},{2,6},{4,0},{6,2},{8,12},{10,14},{12,8},{14,10},{16,20},{18,... | collective-permute-start | bytes 196616 | tf_op jit(solution)/shard_map/ppermute | solution.py:29
  9.1 8.1 %collective-permute-start.5 = (bf16[32,1024]{1,0:T(8,128)(2,1)S(1)}, bf16[32,1024]{1,0:T(8,128)(2,1)S(1)}, u32[]{:S(2)}, u32[]{:S(2)}) collective-permute-start(bf16[32,1024]{1,0:T(8,128)(2,1)S(1)} %add.21), channel_id=1, source_target_pairs={{0,24},{2,26},{4,28},{6,30},{8,16},{10,18},{12,20},{14,22},{16,8},... | collective-permute-start | bytes 196616 | tf_op jit(solution)/shard_map/ppermute | solution.py:29
  12.8 5.3 %collective-permute-start.4 = (bf16[32,1024]{1,0:T(8,128)(2,1)S(1)}, bf16[32,1024]{1,0:T(8,128)(2,1)S(1)}, u32[]{:S(2)}, u32[]{:S(2)}) collective-permute-start(bf16[32,1024]{1,0:T(8,128)(2,1)S(1)} %add.21), channel_id=1, source_target_pairs={{0,16},{2,18},{4,20},{6,22},{8,24},{10,26},{12,28},{14,30},{16,0},... | collective-permute-start | bytes 196616 | tf_op jit(solution)/shard_map/ppermute | solution.py:29
  12.8 5.3 %collective-permute-start.3 = (bf16[32,1024]{1,0:T(8,128)(2,1)S(1)}, bf16[32,1024]{1,0:T(8,128)(2,1)S(1)}, u32[]{:S(2)}, u32[]{:S(2)}) collective-permute-start(bf16[32,1024]{1,0:T(8,128)(2,1)S(1)} %add.21), channel_id=1, source_target_pairs={{0,8},{2,10},{4,12},{6,14},{8,0},{10,2},{12,4},{14,6},{16,24},{18,... | collective-permute-start | bytes 196616 | tf_op jit(solution)/shard_map/ppermute | solution.py:29
  18.1 1.3 %collective-permute-start.6 = (bf16[32,1024]{1,0:T(8,128)(2,1)S(1)}, bf16[32,1024]{1,0:T(8,128)(2,1)S(1)}, u32[]{:S(2)}, u32[]{:S(2)}) collective-permute-start(bf16[32,1024]{1,0:T(8,128)(2,1)S(1)} %add_add_fusion.qa_ref), channel_id=1, source_target_pairs={{0,2},{2,0},{4,6},{6,4},{8,10},{10,8},{12,14},{14,12},{16,18},{18,... | collective-permute-start | bytes 196616 | tf_op jit(solution)/shard_map/ppermute | solution.py:29

commit v3 on v2

--- a/solution.py
+++ b/solution.py
@@ -29,45 +29,50 @@
     return lax.ppermute(values, axis, [(i, i ^ distance) for i in range(count)])
 
 
-def front_kernel(rank_ref, window_hbm, keep_ref, give_ref, sems):
-    half = keep_ref.shape[0]
-    bit = rank_ref[0] % 2
-    copies = [
-        pltpu.make_async_copy(window_hbm.at[pl.ds(pl.multiple_of(which * half, half), half)], ref, sems.at[n])
-        for n, (which, ref) in enumerate(((bit, keep_ref), (1 - bit, give_ref)))
-    ]
+def front_kernel(axis, window_hbm, wf_hbm, wm_hbm, wl_hbm, mine_ref, wf_ref, wm_ref, wl_ref, sems):
+    half = mine_ref.shape[0]
+    rows = pl.ds(pl.multiple_of(lax.axis_index(axis) % 2 * half, half), half)
+    pairs = ((window_hbm.at[rows], mine_ref), (wf_hbm, wf_ref), (wm_hbm, wm_ref), (wl_hbm, wl_ref))
+    copies = [pltpu.make_async_copy(src, dst, sems.at[n]) for n, (src, dst) in enumerate(pairs)]
     for copy in copies:
         copy.start()
     for copy in copies:
         copy.wait()
 
 
-def spread(window, owner, axis):
+def spread(window, owner, axis, target, weights, expand, rest):
     count = lax.axis_size(axis)
     rank = lax.axis_index(axis)
-    half = jax.ShapeDtypeStruct((window.shape[0] // 2, window.shape[1]), window.dtype)
-    keep, give = pl.pallas_call(
-        front_kernel,
-        out_shape=(half, half),
-        in_specs=[SMEM, HBM],
-        out_specs=(VMEM, VMEM),
-        scratch_shapes=[pltpu.SemaphoreType.DMA((2,))],
+    half = window.shape[0] // 2
+    theirs = swapped(window, axis, 1)
+    mine, *weights = pl.pallas_call(
+        functools.partial(front_kernel, axis),
+        out_shape=[jax.ShapeDtypeStruct((half, window.shape[1]), window.dtype)]
+        + [jax.ShapeDtypeStruct(w.shape, w.dtype) for w in weights],
+        in_specs=[HBM] * 4,
+        out_specs=[VMEM] * 4,
+        scratch_shapes=[pltpu.SemaphoreType.DMA((4,))],
         compiler_params=pltpu.CompilerParams(vmem_limit_bytes=VMEM_LIMIT),
         name="front",
-    )(rank.reshape(1), in_hbm(window))
-    held = jnp.where(rank == owner, keep, swapped(give, axis, 1))
-    held = jnp.where(rank // 2 == owner // 2, held, jnp.zeros_like(held))
+    )(in_hbm(window), *(in_hbm(w) for w in weights))
+    expanded = expand(*weights)
+    mine, target, owner = lax.optimization_barrier((mine, target, owner))
+    other = swapped(target, "trow", 1)
+    owner = owner[0]
+    theirs = lax.dynamic_slice_in_dim(theirs, rank % 2 * half, half, 0)
+    sibling = owner + 1 - 2 * (owner % 2)
+    held = jnp.where(rank == owner, mine, jnp.where(rank == sibling, theirs, jnp.zeros_like(mine)))
     bits = [1 << b for b in range(1, count.bit_length() - 1)]
-    rounds = []
-    if len(bits) % 2:
-        rounds.append(bits[:1])
-        bits = bits[1:]
-    for at in range(0, len(bits), 2):
-        low, high = bits[at : at + 2]
-        rounds.append([low, high, low + high])
-    for distances in rounds:
+    rounds = [bits[at : at + 2] for at in range(0, len(bits), 2)]
+    for n, near in enumerate(rounds):
+        distances = near if len(near) == 1 else [sum(near), *near[::-1]]
         held = held + sum(swapped(held, axis, d) for d in distances)
-    return held, swapped(held, axis, 1)
+        if n == 0:
+            held, expanded, rest = lax.optimization_barrier((held, expanded, rest))
+    b_last, valid_rows = rest
+    rest = jnp.where(iota((8, 128), 0) == 0, b_last[0], valid_rows[0].astype(F32))
+    held, rest = lax.optimization_barrier((held, rest))
+    return held, swapped(held, axis, 1), other, expanded, rest
 
 
 def in_hbm(array):
@@ -91,30 +96,13 @@
 
 
 def expand_kernel(
-    ch, misc_ref, wf_hbm, wm_hbm, wl_hbm, w1_ref, w2_ref, w3_ref, rows_ref, wf_ref, wm_ref, wl_ref, sems
+    ch, wf_ref, wm_ref, wl_ref, b1_hbm, b2_hbm, w1_ref, w2_ref, w3_ref, rows_ref, b1_ref, b2_ref, sems
 ):
     group = 2 * ch
-    pairs = ((wf_hbm, wf_ref), (wm_hbm, wm_ref), (wl_hbm, wl_ref))
+    pairs = ((b1_hbm, b1_ref), (b2_hbm, b2_ref))
     copies = [pltpu.make_async_copy(src, dst, sems.at[n]) for n, (src, dst) in enumerate(pairs)]
     for copy in copies:
         copy.start()
-
-    misc = misc_ref[...]
-    chan = iota((8, 128), 1)
-    for n in range(2):
-        total = jnp.where(chan < ch, pltpu.roll(misc, 128 - n * ch, 1) if n else misc, 0.0)
-        size = ch
-        while size < 128:
-            total = total + pltpu.roll(total, size, 1)
-            size *= 2
-        rows_ref[n : n + 1, 0:128] = total[0:1]
-        rows_ref[n : n + 1, 128:256] = total[0:1]
-    for n in range(2):
-        at = 2 * ch + n
-        rows_ref[2 + n : 3 + n, :] = jnp.broadcast_to(misc[0:1, at : at + 1], (1, 256))
-
-    for copy in copies:
-        copy.wait()
 
     def by_offset(ref):
         values = ref[...].astype(F32)
@@ -132,9 +120,9 @@
             l, rp, j = lane // 6, (lane // 3) % 2, lane % 3
             want = l * 32 + ((rp - ra + 1) * 3 + j) * 3 + k
             base.append(dot(taps, one_hot((src == want) & (lane < 18))))
-    base = jnp.concatenate(base, axis=0).astype(BF16)
-    row = iota((128, 256), 0)
-    col = iota((128, 256), 1)
+    base = jnp.concatenate(base, axis=0).astype(BF16)[:, :32]
+    row = iota((32, 256), 0)
+    col = iota((32, 256), 1)
     l, rp, j = row // 6, (row // 3) % 2, row % 3
     for ca in range(WA):
         at = ca + j - 1
@@ -155,18 +143,31 @@
             part = dot(picked, one_hot(col == j * group + rp * ch + row))
             total = part if total is None else total + part
     base = total.astype(BF16)
-    row = iota((128, 256), 0)
-    col = iota((128, 256), 1)
-    moves = [one_hot((col == row + group * b) & (row < 3 * group)) for b in range(4)]
-    moved = [dot(base, m).astype(BF16) for m in moves]
+    row = iota((128, 128), 0)
+    col = iota((128, 128), 1)
+    inner = [dot(base, one_hot((col == row + group * (ca - 1)) & (row < 3 * group))).astype(BF16) for ca in range(4)]
+    outer = {
+        (side, half): dot(
+            base, one_hot((col == row + half * 64 + (-group if side else 0)) & (row // group == 2 * side))
+        ).astype(BF16)
+        for side in range(2)
+        for half in range(2)
+    }
+    left = iota((group, 128), 1) < 64
     blank = jnp.zeros((group, 128), BF16)
-    for tap in range(9):
-        for ca in range(8):
-            a, b = divmod(ca + 3, 4)
-            piece = moved[b][tap * group : (tap + 1) * group]
-            for v in range(4):
-                chunk = piece[:, :128] if v == a else piece[:, 128:] if v == a + 1 else blank
-                w2_ref[tap, ca * group : (ca + 1) * group, v * 128 : (v + 1) * 128] = chunk
+    for k in range(3):
+        tap = lambda values, l: values[(k * 3 + l) * group : (k * 3 + l + 1) * group] if 0 <= l < 3 else blank
+        for u in range(2):
+            for ca in range(4):
+                rows = slice((u * 4 + ca) * group, (u * 4 + ca + 1) * group)
+                for slab in range(4):
+                    w2_ref[k, rows, slab * 128 : (slab + 1) * 128] = tap(inner[ca], slab - u)
+                for v in range(2):
+                    piece = blank
+                    if ca in (0, 3):
+                        side = ca // 3
+                        piece = jnp.where(left, tap(outer[side, 0], 2 * v - u), tap(outer[side, 1], 2 * v + 1 - u))
+                    w2_ref[k, rows, 512 + v * 128 : 640 + v * 128] = piece
 
     taps = by_offset(wl_ref).astype(BF16)
     out_row = iota((24, 96), 0)
@@ -182,7 +183,9 @@
             part = dot(picked, one_hot(col == j * group + rp * ch + row))
             total = part if total is None else total + part
     base = total.astype(BF16)
-    moved = [dot(base, m) for m in moves]
+    row = iota((128, 256), 0)
+    col = iota((128, 256), 1)
+    moved = [dot(base, one_hot((col == row + group * b) & (row < 3 * group))) for b in range(4)]
     blank = jnp.zeros((8, 128), F32)
     lanes = WA * group // 128
     for k in range(3):
@@ -197,13 +200,23 @@
                     chunks, axis=0
                 ).astype(BF16)
 
+    for copy in copies:
+        copy.wait()
+
+    chan = iota((1, 256), 1) % ch
+    for n, ref in enumerate((b1_ref, b2_ref)):
+        total = jnp.zeros((1, 256), F32)
+        for o in range(ch):
+            total = jnp.where(chan == o, ref[o], total)
+        rows_ref[n : n + 1, :] = total
+
 
 def score_kernel(
-    rows_here, n1, n2, s_ref, rows_ref, tm_ref, to_ref, qa_ref, qb_ref, w1_ref, w2_ref, w3_ref,
-    out_ref, v_ref, x_ref, h1_ref, h2_ref, ya_ref, yb_ref, yt_ref,
+    rows_here, n1, n2, rest_ref, rows_ref, tm_ref, to_ref, qa_ref, qb_ref, w1_ref, w2_ref, w3_ref,
+    out_ref, v_ref, x_ref, h1_ref, e_ref, h2_ref, ya_ref, yb_ref, yt_ref,
 ):
-    trow, bit = s_ref[0], s_ref[1]
-    count = rows_ref[3:4, :]
+    trow, bit = lax.axis_index("trow"), lax.axis_index("pair") % 2
+    count = rest_ref[1:2, :]
     cells = tm_ref.shape[0]
     grid_rows = cells // WB
     width = tm_ref.shape[1]
@@ -230,7 +243,7 @@
         return jnp.sum(values * values, axis=1, keepdims=True)
 
     inv = lax.rsqrt(squares(tm_ref) + squares(to_ref) + EPS_NORM)
-    live = (iota((cells, 128), 0) // WB).astype(F32) < count[:, :128]
+    live = (iota((cells, 128), 0) // WB).astype(F32) < count
     corr = jnp.where(live, scale * raw * inv, 0.0)
     mag = jnp.abs(corr)
     peak_query = jnp.max(mag, axis=1, keepdims=True)
@@ -276,16 +289,40 @@
         h1_ref[1 : n1 + 1, 0:half, cols] = before.reshape(n1, half, 256).astype(BF16)
         h1_ref[1 : n1 + 1, half + WB :, cols] = after.reshape(n1, half, 256).astype(BF16)
 
+    lane = iota((n1, half, 128), 2)
+    blank = jnp.zeros((n1, half, 128), BF16)
+    blocks = lanes // 128
+    e_ref[0] = jnp.zeros((half, 2 * lanes), BF16)
+    e_ref[n1 + 1] = jnp.zeros((half, 2 * lanes), BF16)
+
+    def turned(slab, block):
+        if not 0 <= block < blocks:
+            return blank
+        values = h1_ref[1 : n1 + 1, slab * half : (slab + 1) * half, block * 128 : (block + 1) * 128]
+        return pltpu.roll(values.reshape(n1 * half, 128), 96 if slab % 2 else 32, 1).reshape(n1, half, 128)
+
+    for v in range(2):
+        for q in range(blocks):
+            one, two = 2 * v, 2 * v + 1
+            first = jnp.where(lane < 32, turned(one, q - 1), turned(one, q + 1))
+            second = jnp.where(lane < 96, turned(two, q - 1), turned(two, q + 1))
+            e_ref[1 : n1 + 1, :, q * 256 + v * 128 : q * 256 + v * 128 + 128] = jnp.where(lane < 64, first, second)
+
     off2 = start2 - start1
-    for q in range(lanes // 256):
-        cols = slice(q * 256, (q + 1) * 256)
-        lo, hi = max(q * 256 - 128, 0), min(q * 256 + 384, lanes)
+    for q0 in range(0, blocks, 2):
         total = bias2
         for k in range(3):
-            for l in range(3):
-                cells_in = h1_ref[pl.ds(off2 + k, n2), l * half : l * half + WB, lo:hi].reshape(n2 * WB, hi - lo)
-                total = total + dot_nt(cells_in, w2_ref[k * 3 + l, :, lo - q * 256 + 128 : hi - q * 256 + 128])
-        h2_ref[1 : n2 + 1, :, cols] = jnp.maximum(total, 0.0).reshape(n2, WB, 256).astype(BF16)
+            rows = pl.ds(off2 + k, n2)
+            stack = []
+            for q in range(q0, q0 + 2):
+                parts = [h1_ref[rows, o * half : (o + 1) * half, q * 128 : (q + 1) * 128] for o in range(4)]
+                parts.append(e_ref[rows, :, q * 256 : (q + 1) * 256])
+                stack.append(jnp.concatenate([p.reshape(n2 * half, p.shape[2]) for p in parts], axis=1))
+            total = total + dot_nt(jnp.concatenate(stack, axis=0), w2_ref[k])
+        total = jnp.maximum(total, 0.0).reshape(2, n2, half, 256).astype(BF16)
+        for q in range(q0, q0 + 2):
+            for u in range(2):
+                h2_ref[1 : n2 + 1, u * half : (u + 1) * half, q * 128 : (q + 1) * 128] = total[q - q0, :, :, u * 128 : (u + 1) * 128]
 
     off3 = rows_here * trow - start2
     total = None
@@ -310,7 +347,7 @@
         ]
         before = jnp.where(lane % WB == 0, 0.0, pltpu.roll(parts[0], 1, 1))
         after = jnp.where(lane % WB == WB - 1, 0.0, pltpu.roll(parts[2], here - 1, 1))
-        result = before + parts[1] + after + rows_ref[2:3, :1]
+        result = before + parts[1] + after + rest_ref[0:1, :1]
         out_ref[0, ra * WA : (ra + 1) * WA, :] = jnp.where(keep, result, 0.0)
 
 
@@ -329,45 +366,43 @@
     sides = 1 if trows == 2 else 2
     n1, n2 = min(rows_here + 2 * sides, grid_rows), min(rows_here + sides, grid_rows)
 
-    other = swapped(target, "trow", 1)
-    own, sibling = spread(query_bank[0], ref_owner[0], "pair")
-    ranks = jnp.stack([lax.axis_index("trow"), lax.axis_index("pair") % 2]).astype(jnp.int32)
-
-    misc = jnp.concatenate([b_first, b_middle, b_last, valid_rows.astype(F32)])
-    w1, w2, w3, rows = pl.pallas_call(
+    expand = pl.pallas_call(
         functools.partial(expand_kernel, ch),
         out_shape=(
             jax.ShapeDtypeStruct((3, lanes, 256), BF16),
-            jax.ShapeDtypeStruct((9, 256, 512), BF16),
+            jax.ShapeDtypeStruct((3, 256, 768), BF16),
             jax.ShapeDtypeStruct((3, 256, lanes), BF16),
             jax.ShapeDtypeStruct((8, 256), F32),
         ),
-        in_specs=[VMEM] + [HBM] * 3,
+        in_specs=[VMEM] * 3 + [HBM] * 2,
         out_specs=(VMEM,) * 4,
         scratch_shapes=[
-            pltpu.VMEM((27, 3, ch), BF16),
-            pltpu.VMEM((81, ch, ch), BF16),
-            pltpu.VMEM((27, 3, ch), BF16),
-            pltpu.SemaphoreType.DMA((3,)),
+            pltpu.SMEM((ch,), F32),
+            pltpu.SMEM((ch,), F32),
+            pltpu.SemaphoreType.DMA((2,)),
         ],
         compiler_params=pltpu.CompilerParams(vmem_limit_bytes=VMEM_LIMIT),
         name="expand",
-    )(
-        jnp.broadcast_to(jnp.pad(misc, (0, 128 - misc.shape[0])), (8, 128)),
-        in_hbm(jnp.transpose(w_first, (1, 2, 3, 4, 5, 0)).reshape(27, 3, ch)),
-        in_hbm(jnp.transpose(w_middle, (2, 3, 4, 5, 0, 1)).reshape(81, ch, ch)),
-        in_hbm(jnp.transpose(w_last, (0, 2, 3, 4, 5, 1)).reshape(27, 3, ch)),
     )
-
+    weights = (
+        jnp.transpose(w_first, (1, 2, 3, 4, 5, 0)).reshape(27, 3, ch),
+        jnp.transpose(w_middle, (2, 3, 4, 5, 0, 1)).reshape(81, ch, ch),
+        jnp.transpose(w_last, (0, 2, 3, 4, 5, 1)).reshape(27, 3, ch),
+    )
+    biased = lambda *taps: expand(*taps, in_hbm(b_first), in_hbm(b_middle))
+    own, sibling, other, (w1, w2, w3, rows), rest = spread(
+        query_bank[0], ref_owner, "pair", target, weights, biased, (b_last, valid_rows)
+    )
     return pl.pallas_call(
         functools.partial(score_kernel, rows_here, n1, n2),
         out_shape=jax.ShapeDtypeStruct((1, positions, rows_here * WB), F32),
-        in_specs=[SMEM] + [VMEM] * 8,
+        in_specs=[VMEM] * 9,
         out_specs=VMEM,
         scratch_shapes=[
             pltpu.VMEM((8 + (grid_rows + 2) * PITCH, 128), F32),
             pltpu.VMEM((n1 + 2, WB, 256), BF16),
             pltpu.VMEM((n1 + 2, 2 * WB, lanes), BF16),
+            pltpu.VMEM((n1 + 2, WB // 2, 2 * lanes), BF16),
             pltpu.VMEM((n2 + 2, WB, lanes), BF16),
             pltpu.VMEM((rows_here * WB, 128), F32),
             pltpu.VMEM((rows_here * WB, 128), F32),
@@ -375,7 +410,7 @@
         ],
         compiler_params=pltpu.CompilerParams(vmem_limit_bytes=VMEM_LIMIT),
         name="score",
-    )(ranks, rows, target, other, own, sibling, w1, w2, w3)
+    )(rest, rows, target, other, own, sibling, w1, w2, w3)
 
 
 def solution(mesh):

time: 26.5 us -> 24 us (0.906)
  Pallas kernels: 10.7 us -> 8.27 us
  other arithmetic: 0.88 us -> 0.06 us
  waiting for transfers between devices: 3.55 us -> 4.04 us
    pallas_call x1, Pallas kernels: 6.88 us -> 5.02 us  [per_device(): pl.pallas_call(functools.partial(score_kernel, rows_here, n1, n2), out_sh...]
    concatenate x1 -> x0, other arithmetic: 0.75 us -> none  [per_device(): misc = jnp.concatenate([b_first, b_middle, b_last, valid_rows.astype(F32)])]
    pallas_call x2, Pallas kernels: 3.78 us -> 3.25 us  [the longest x1 2.18 us: per_device(): biased = lambda *taps: expand(*taps, in_hbm(b_first), in_hbm(b_middle))]
    ppermute x7, waiting for transfers between devices: 3.55 us -> 4.04 us  [swapped(): return lax.ppermute(values, axis, [(i, i ^ distance) for i in range(count)])]
  transfers between devices with their start and end apart: 7 -> 7, of which waited for: 3 -> 3; matrix products, arithmetic and copies ran while one was open for 3% -> 1% of each run, Pallas kernels for 11% -> 14%
where the time goes in v3:
time: 24 us; the launch traced here: 23.8 us
  starting transfers between devices  9.32 us (39%)
  Pallas kernels  8.27 us (34%)
  waiting for transfers between devices  4.04 us (17%)
  between operations  2.05 us (9%)
    ppermute x7, starting transfers between devices, swapped(): return lax.ppermute(values, axis, [(i, i ^ distance) for i in range(count)])  9.32 us
    pallas_call x1, Pallas kernels, per_device(): pl.pallas_call(functools.partial(score_kernel, rows_here, n1, n2), out_sh...  5.02 us
    ppermute x7, waiting for transfers between devices, swapped(): return lax.ppermute(values, axis, [(i, i ^ distance) for i in range(count)])  4.04 us
    pallas_call x1, Pallas kernels, per_device(): biased = lambda *taps: expand(*taps, in_hbm(b_first), in_hbm(b_middle))  2.18 us
    pallas_call x1, Pallas kernels, spread(): pl.pallas_call(functools.partial(front_kernel, axis), out_shape=[jax.Shap...  1.07 us
  transfers between devices with their start and end apart: 7, of which 3 were waited for; matrix products, arithmetic and copies ran while one was open for 1% of the time, Pallas kernels for 14%

profile of v3, /device:TPU:0, one launch (start us, length us, event | category | flops | bytes accessed | tf_op | source)
XLA Modules:
  0.0 23.8 jit_solution(17528274216704602881)
XLA Ops:
  0.0 0.0 copy-start
  0.0 0.5 %collective-permute-start = (bf16[64,1024]{1,0:T(8,128)(2,1)}, bf16[64,1024]{1,0:T(8,128)(2,1)S(1)}, u32[]{:S(2)}, u32[]{:S(2)}) collective-permute-start(bf16[64,1024]{1,0:T(8,128)(2,1)} %bitcast.23), channel_id=1, source_target_pairs={{0,2},{2,0},{4,6},{6,4},{8,10},{10,8},{12,14},{14,12},{16,18},{18,... | collective-permute-start | bytes 393224 | tf_op jit(solution)/shard_map/ppermute | solution.py:29
  0.5 1.1 %front.1 = (bf16[32,1024]{1,0:T(8,128)(2,1)S(1)}, bf16[27,3,16]{2,1,0:T(4,128)(2,1)S(1)}, bf16[81,16,16]{2,1,0:T(8,128)(2,1)S(1)}, bf16[27,3,16]{2,1,0:T(4,128)(2,1)S(1)}) custom-call(bf16[64,1024]{1,0:T(8,128)(2,1)} %bitcast.24, bf16[27,3,16]{2,1,0:T(4,128)(2,1)} %bitcast.25, bf16[81,16,16]{2,1,0:T(8,128)(2,1)} %bitcast.22, bf16[27,3,16]{2,1,0:T(4,128)(2,1)} %bitcast.26), custom_call_target="tpu_custom_call" | custom-call | tf_op jit(solution)/shard_map/front/pallas_call | solution.py:48
  1.5 2.6 %collective-permute-start.5 = (bf16[512,512]{1,0:T(8,128)(2,1)}, bf16[512,512]{1,0:T(8,128)(2,1)S(1)}, u32[]{:S(2)}, u32[]{:S(2)}) collective-permute-start(bf16[512,512]{1,0:T(8,128)(2,1)} %bitcast.20), channel_id=1, source_target_pairs={{0,1},{1,0},{2,3},{3,2},{4,5},{5,4},{6,7},{7,6},{8,9},{9,8},{10,11... | collective-permute-start | bytes 1572872 | tf_op jit(solution)/shard_map/ppermute | solution.py:29
  4.9 0.0 collective-permute-done
  4.9 2.6 %collective-permute-start.1 = (bf16[32,1024]{1,0:T(8,128)(2,1)S(1)}, bf16[32,1024]{1,0:T(8,128)(2,1)S(1)}, u32[]{:S(2)}, u32[]{:S(2)}) collective-permute-start(bf16[32,1024]{1,0:T(8,128)(2,1)S(1)} %select_select_fusion), channel_id=1, source_target_pairs={{0,12},{2,14},{4,8},{6,10},{8,4},{10,6},{12,0},{14,2},{16,28},{18,... | collective-permute-start | bytes 196616 | tf_op jit(solution)/shard_map/ppermute | solution.py:29
  7.5 0.4 %collective-permute-start.2 = (bf16[32,1024]{1,0:T(8,128)(2,1)S(1)}, bf16[32,1024]{1,0:T(8,128)(2,1)S(1)}, u32[]{:S(2)}, u32[]{:S(2)}) collective-permute-start(bf16[32,1024]{1,0:T(8,128)(2,1)S(1)} %select_select_fusion), channel_id=1, source_target_pairs={{0,8},{2,10},{4,12},{6,14},{8,0},{10,2},{12,4},{14,6},{16,24},{18,... | collective-permute-start | bytes 196616 | tf_op jit(solution)/shard_map/ppermute | solution.py:29
  7.9 0.5 %collective-permute-start.3 = (bf16[32,1024]{1,0:T(8,128)(2,1)S(1)}, bf16[32,1024]{1,0:T(8,128)(2,1)S(1)}, u32[]{:S(2)}, u32[]{:S(2)}) collective-permute-start(bf16[32,1024]{1,0:T(8,128)(2,1)S(1)} %select_select_fusion), channel_id=1, source_target_pairs={{0,4},{2,6},{4,0},{6,2},{8,12},{10,14},{12,8},{14,10},{16,20},{18,... | collective-permute-start | bytes 196616 | tf_op jit(solution)/shard_map/ppermute | solution.py:29
  9.8 2.2 %expand.1 = (bf16[3,1024,256]{2,1,0:T(8,128)(2,1)S(1)}, bf16[3,256,768]{2,1,0:T(8,128)(2,1)S(1)}, bf16[3,256,1024]{2,1,0:T(8,128)(2,1)S(1)}, f32[8,256]{1,0:T(8,128)S(1)}) custom-call(bf16[27,3,16]{2,1,0:T(4,128)(2,1)S(1)} %get-tuple-element.28.wf_ref, bf16[81,16,16]{2,1,0:T(8,128)(2,1)S(1)} %get-tuple-element.29.wm_ref, ...), custom_call_target="tpu_custom_call" | custom-call | tf_op jit(solution)/shard_map/expand/pallas_call | solution.py:392
  11.9 0.0 collective-permute-done.1
  12.0 0.0 collective-permute-done.2
  12.0 0.2 collective-permute-done.3
  12.2 2.7 %collective-permute-start.4 = (bf16[32,1024]{1,0:T(8,128)(2,1)S(1)}, bf16[32,1024]{1,0:T(8,128)(2,1)S(1)}, u32[]{:S(2)}, u32[]{:S(2)}) collective-permute-start(bf16[32,1024]{1,0:T(8,128)(2,1)S(1)} %add_add_fusion), channel_id=1, source_target_pairs={{0,16},{2,18},{4,20},{6,22},{8,24},{10,26},{12,28},{14,30},{16,0},... | collective-permute-start | bytes 196616 | tf_op jit(solution)/shard_map/ppermute | solution.py:29
  14.9 2.6 %collective-permute-done.4 = bf16[32,1024]{1,0:T(8,128)(2,1)S(1)} collective-permute-done((bf16[32,1024]{1,0:T(8,128)(2,1)S(1)}, bf16[32,1024]{1,0:T(8,128)(2,1)S(1)}, u32[]{:S(2)}, u32[]{:S(2)}) %collective-permute-start.4) | collective-permute-done | bytes 65568 | tf_op jit(solution)/shard_map/ppermute | solution.py:29
  17.5 0.1 iota.7.rest_ref
  17.5 0.0 collective-permute-start.6
  17.5 1.2 %collective-permute-done.6.qb_ref = bf16[32,1024]{1,0:T(8,128)(2,1)S(1)} collective-permute-done((bf16[32,1024]{1,0:T(8,128)(2,1)S(1)}, bf16[32,1024]{1,0:T(8,128)(2,1)S(1)}, u32[]{:S(2)}, u32[]{:S(2)}) %collective-permute-start.6) | collective-permute-done | bytes 65568 | tf_op jit(solution)/shard_map/ppermute | solution.py:29
  18.8 0.0 collective-permute-done.5.to_ref
  18.8 0.0 copy-done
  18.8 5.0 %score.1 = f32[1,64,256]{2,1,0:T(8,128)} custom-call(f32[8,128]{1,0:T(8,128)S(1)} %iota.7.rest_ref, f32[8,256]{1,0:T(8,128)S(1)} %get-tuple-element.39.rows_ref, bf16[512,512]{1,0:T(8,128)(2,1)S(1)} %bitcast.21, bf16[512,512]{1,0:T(8,128)(2,1)S(1)} %collective-permute-done.5.to_ref, bf16[32,1024]{1,0:T(8,128)(2,1)S(1)} %add.32.qa_ref, ...), custom_call_target="tpu_custom_call" | custom-call | tf_op jit(solution)/shard_map/score/pallas_call | solution.py:396
  (4 shorter events, 0.1 us)
Async XLA Ops:
  0.0 18.8 %copy-start = (bf16[1,512,512]{2,1,0:T(8,128)(2,1)S(1)}, bf16[1,512,512]{2,1,0:T(8,128)(2,1)}, u32[]{:S(2)}) copy-start(bf16[1,512,512]{2,1,0:T(8,128)(2,1)} %param.12) | copy-start | bytes 1572868
  0.0 4.9 %collective-permute-start = (bf16[64,1024]{1,0:T(8,128)(2,1)}, bf16[64,1024]{1,0:T(8,128)(2,1)S(1)}, u32[]{:S(2)}, u32[]{:S(2)}) collective-permute-start(bf16[64,1024]{1,0:T(8,128)(2,1)} %bitcast.23), channel_id=1, source_target_pairs={{0,2},{2,0},{4,6},{6,4},{8,10},{10,8},{12,14},{14,12},{16,18},{18,... | collective-permute-start | bytes 393224 | tf_op jit(solution)/shard_map/ppermute | solution.py:29
  1.5 17.3 %collective-permute-start.5 = (bf16[512,512]{1,0:T(8,128)(2,1)}, bf16[512,512]{1,0:T(8,128)(2,1)S(1)}, u32[]{:S(2)}, u32[]{:S(2)}) collective-permute-start(bf16[512,512]{1,0:T(8,128)(2,1)} %bitcast.20), channel_id=1, source_target_pairs={{0,1},{1,0},{2,3},{3,2},{4,5},{5,4},{6,7},{7,6},{8,9},{9,8},{10,11... | collective-permute-start | bytes 1572872 | tf_op jit(solution)/shard_map/ppermute | solution.py:29
  4.9 7.0 %collective-permute-start.1 = (bf16[32,1024]{1,0:T(8,128)(2,1)S(1)}, bf16[32,1024]{1,0:T(8,128)(2,1)S(1)}, u32[]{:S(2)}, u32[]{:S(2)}) collective-permute-start(bf16[32,1024]{1,0:T(8,128)(2,1)S(1)} %select_select_fusion), channel_id=1, source_target_pairs={{0,12},{2,14},{4,8},{6,10},{8,4},{10,6},{12,0},{14,2},{16,28},{18,... | collective-permute-start | bytes 196616 | tf_op jit(solution)/shard_map/ppermute | solution.py:29
  7.5 4.5 %collective-permute-start.2 = (bf16[32,1024]{1,0:T(8,128)(2,1)S(1)}, bf16[32,1024]{1,0:T(8,128)(2,1)S(1)}, u32[]{:S(2)}, u32[]{:S(2)}) collective-permute-start(bf16[32,1024]{1,0:T(8,128)(2,1)S(1)} %select_select_fusion), channel_id=1, source_target_pairs={{0,8},{2,10},{4,12},{6,14},{8,0},{10,2},{12,4},{14,6},{16,24},{18,... | collective-permute-start | bytes 196616 | tf_op jit(solution)/shard_map/ppermute | solution.py:29
  7.9 4.3 %collective-permute-start.3 = (bf16[32,1024]{1,0:T(8,128)(2,1)S(1)}, bf16[32,1024]{1,0:T(8,128)(2,1)S(1)}, u32[]{:S(2)}, u32[]{:S(2)}) collective-permute-start(bf16[32,1024]{1,0:T(8,128)(2,1)S(1)} %select_select_fusion), channel_id=1, source_target_pairs={{0,4},{2,6},{4,0},{6,2},{8,12},{10,14},{12,8},{14,10},{16,20},{18,... | collective-permute-start | bytes 196616 | tf_op jit(solution)/shard_map/ppermute | solution.py:29
  12.2 5.2 %collective-permute-start.4 = (bf16[32,1024]{1,0:T(8,128)(2,1)S(1)}, bf16[32,1024]{1,0:T(8,128)(2,1)S(1)}, u32[]{:S(2)}, u32[]{:S(2)}) collective-permute-start(bf16[32,1024]{1,0:T(8,128)(2,1)S(1)} %add_add_fusion), channel_id=1, source_target_pairs={{0,16},{2,18},{4,20},{6,22},{8,24},{10,26},{12,28},{14,30},{16,0},... | collective-permute-start | bytes 196616 | tf_op jit(solution)/shard_map/ppermute | solution.py:29
  17.5 1.3 %collective-permute-start.6 = (bf16[32,1024]{1,0:T(8,128)(2,1)S(1)}, bf16[32,1024]{1,0:T(8,128)(2,1)S(1)}, u32[]{:S(2)}, u32[]{:S(2)}) collective-permute-start(bf16[32,1024]{1,0:T(8,128)(2,1)S(1)} %add.32.qa_ref), channel_id=1, source_target_pairs={{0,2},{2,0},{4,6},{6,4},{8,10},{10,8},{12,14},{14,12},{16,18},{18,... | collective-permute-start | bytes 196616 | tf_op jit(solution)/shard_map/ppermute | solution.py:29

commit v4 on v3

--- a/solution.py
+++ b/solution.py
@@ -29,10 +29,8 @@
     return lax.ppermute(values, axis, [(i, i ^ distance) for i in range(count)])
 
 
-def front_kernel(axis, window_hbm, wf_hbm, wm_hbm, wl_hbm, mine_ref, wf_ref, wm_ref, wl_ref, sems):
-    half = mine_ref.shape[0]
-    rows = pl.ds(pl.multiple_of(lax.axis_index(axis) % 2 * half, half), half)
-    pairs = ((window_hbm.at[rows], mine_ref), (wf_hbm, wf_ref), (wm_hbm, wm_ref), (wl_hbm, wl_ref))
+def fetch_kernel(wf_hbm, wm_hbm, wl_hbm, wf_ref, wm_ref, wl_ref, sems):
+    pairs = ((wf_hbm, wf_ref), (wm_hbm, wm_ref), (wl_hbm, wl_ref))
     copies = [pltpu.make_async_copy(src, dst, sems.at[n]) for n, (src, dst) in enumerate(pairs)]
     for copy in copies:
         copy.start()
@@ -40,38 +38,56 @@
         copy.wait()
 
 
+def front_kernel(axis, window_hbm, mine_ref, sem):
+    half = mine_ref.shape[0]
+    rows = pl.ds(pl.multiple_of(lax.axis_index(axis) % 2 * half, half), half)
+    copy = pltpu.make_async_copy(window_hbm.at[rows], mine_ref, sem)
+    copy.start()
+    copy.wait()
+
+
 def spread(window, owner, axis, target, weights, expand, rest):
     count = lax.axis_size(axis)
     rank = lax.axis_index(axis)
     half = window.shape[0] // 2
     theirs = swapped(window, axis, 1)
-    mine, *weights = pl.pallas_call(
+    fetch = pl.pallas_call(
+        fetch_kernel,
+        out_shape=[jax.ShapeDtypeStruct(w.shape, w.dtype) for w in weights],
+        in_specs=[HBM] * 3,
+        out_specs=[VMEM] * 3,
+        scratch_shapes=[pltpu.SemaphoreType.DMA((3,))],
+        compiler_params=pltpu.CompilerParams(vmem_limit_bytes=VMEM_LIMIT),
+        name="fetch",
+    )
+    mine = pl.pallas_call(
         functools.partial(front_kernel, axis),
-        out_shape=[jax.ShapeDtypeStruct((half, window.shape[1]), window.dtype)]
-        + [jax.ShapeDtypeStruct(w.shape, w.dtype) for w in weights],
-        in_specs=[HBM] * 4,
-        out_specs=[VMEM] * 4,
-        scratch_shapes=[pltpu.SemaphoreType.DMA((4,))],
+        out_shape=jax.ShapeDtypeStruct((half, window.shape[1]), window.dtype),
+        in_specs=[HBM],
+        out_specs=VMEM,
+        scratch_shapes=[pltpu.SemaphoreType.DMA],
         compiler_params=pltpu.CompilerParams(vmem_limit_bytes=VMEM_LIMIT),
         name="front",
-    )(in_hbm(window), *(in_hbm(w) for w in weights))
-    expanded = expand(*weights)
+    )(in_hbm(window))
     mine, target, owner = lax.optimization_barrier((mine, target, owner))
     other = swapped(target, "trow", 1)
     owner = owner[0]
     theirs = lax.dynamic_slice_in_dim(theirs, rank % 2 * half, half, 0)
     sibling = owner + 1 - 2 * (owner % 2)
     held = jnp.where(rank == owner, mine, jnp.where(rank == sibling, theirs, jnp.zeros_like(mine)))
+    held, weights = lax.optimization_barrier((held, weights))
+    weights = fetch(*(in_hbm(w) for w in weights))
     bits = [1 << b for b in range(1, count.bit_length() - 1)]
     rounds = [bits[at : at + 2] for at in range(0, len(bits), 2)]
     for n, near in enumerate(rounds):
         distances = near if len(near) == 1 else [sum(near), *near[::-1]]
         held = held + sum(swapped(held, axis, d) for d in distances)
         if n == 0:
-            held, expanded, rest = lax.optimization_barrier((held, expanded, rest))
+            held, weights, rest = lax.optimization_barrier((held, weights, rest))
+            expanded = expand(*weights)
     b_last, valid_rows = rest
     rest = jnp.where(iota((8, 128), 0) == 0, b_last[0], valid_rows[0].astype(F32))
-    held, rest = lax.optimization_barrier((held, rest))
+    held, rest, expanded = lax.optimization_barrier((held, rest, expanded))
     return held, swapped(held, axis, 1), other, expanded, rest
 
 
@@ -213,7 +229,7 @@
 
 def score_kernel(
     rows_here, n1, n2, rest_ref, rows_ref, tm_ref, to_ref, qa_ref, qb_ref, w1_ref, w2_ref, w3_ref,
-    out_ref, v_ref, x_ref, h1_ref, e_ref, h2_ref, ya_ref, yb_ref, yt_ref,
+    out_ref, v_ref, x_ref, ya_ref, yb_ref, yt_ref, *layers,
 ):
     trow, bit = lax.axis_index("trow"), lax.axis_index("pair") % 2
     count = rest_ref[1:2, :]
@@ -266,69 +282,85 @@
             x_ref[r, u * half : (u + 1) * half, 0:128] = jnp.where(left, slabs[u], slabs[u + 1]).astype(BF16)
             x_ref[r, u * half : (u + 1) * half, 128:256] = jnp.where(left, slabs[u + 2], 0.0).astype(BF16)
 
-    lanes = h1_ref.shape[2]
-    zero = jnp.zeros((2 * WB, lanes), BF16)
-    h1_ref[0] = zero
-    h1_ref[n1 + 1] = zero
-    h2_ref[0] = zero[:WB]
-    h2_ref[n2 + 1] = zero[:WB]
+    groups = len(layers) // 3
+    h1_refs, e_refs, h2_refs = layers[:groups], layers[groups : 2 * groups], layers[2 * groups :]
+    for ref, count1 in [(r, n1) for r in (*h1_refs, *e_refs)] + [(r, n2) for r in h2_refs]:
+        ref[0] = jnp.zeros(ref.shape[1:], BF16)
+        ref[count1 + 1] = jnp.zeros(ref.shape[1:], BF16)
+    bias1, bias2 = rows_ref[0:1, :], rows_ref[1:2, :]
+    off2 = start2 - start1
+    off3 = rows_here * trow - start2
     step = iota((n1 * half, 256), 0) % half
-    bias1, bias2 = rows_ref[0:1, :], rows_ref[1:2, :]
-    for q in range(lanes // 256):
-        cols = slice(q * 256, (q + 1) * 256)
+
+    def first_layer(g):
+        cols = slice(g * 256, (g + 1) * 256)
         total = bias1
         for k in range(3):
             total = total + dot_nt(x_ref[k : k + n1].reshape(n1 * WB, 256), w1_ref[k, cols, :])
         total = jnp.maximum(total, 0.0)
-        h1_ref[1 : n1 + 1, half : half + WB, cols] = total.reshape(n1, WB, 256).astype(BF16)
+        ref = h1_refs[g]
+        ref[1 : n1 + 1, half : half + WB, :] = total.reshape(n1, WB, 256).astype(BF16)
         parts = total.reshape(n1, 2, half, 256)
         even = parts[:, 0].reshape(n1 * half, 256)
         odd = parts[:, 1].reshape(n1 * half, 256)
         before = jnp.where(step == 0, 0.0, pltpu.roll(odd, 1, 0))
         after = jnp.where(step == half - 1, 0.0, pltpu.roll(even, n1 * half - 1, 0))
-        h1_ref[1 : n1 + 1, 0:half, cols] = before.reshape(n1, half, 256).astype(BF16)
-        h1_ref[1 : n1 + 1, half + WB :, cols] = after.reshape(n1, half, 256).astype(BF16)
+        ref[1 : n1 + 1, 0:half, :] = before.reshape(n1, half, 256).astype(BF16)
+        ref[1 : n1 + 1, half + WB :, :] = after.reshape(n1, half, 256).astype(BF16)
 
     lane = iota((n1, half, 128), 2)
     blank = jnp.zeros((n1, half, 128), BF16)
-    blocks = lanes // 128
-    e_ref[0] = jnp.zeros((half, 2 * lanes), BF16)
-    e_ref[n1 + 1] = jnp.zeros((half, 2 * lanes), BF16)
 
     def turned(slab, block):
-        if not 0 <= block < blocks:
+        if not 0 <= block < 2 * groups:
             return blank
-        values = h1_ref[1 : n1 + 1, slab * half : (slab + 1) * half, block * 128 : (block + 1) * 128]
+        g, part = divmod(block, 2)
+        values = h1_refs[g][1 : n1 + 1, slab * half : (slab + 1) * half, part * 128 : (part + 1) * 128]
         return pltpu.roll(values.reshape(n1 * half, 128), 96 if slab % 2 else 32, 1).reshape(n1, half, 128)
 
-    for v in range(2):
-        for q in range(blocks):
-            one, two = 2 * v, 2 * v + 1
-            first = jnp.where(lane < 32, turned(one, q - 1), turned(one, q + 1))
-            second = jnp.where(lane < 96, turned(two, q - 1), turned(two, q + 1))
-            e_ref[1 : n1 + 1, :, q * 256 + v * 128 : q * 256 + v * 128 + 128] = jnp.where(lane < 64, first, second)
-
-    off2 = start2 - start1
-    for q0 in range(0, blocks, 2):
+    def borders(g):
+        for part in range(2):
+            block = 2 * g + part
+            for v in range(2):
+                one, two = 2 * v, 2 * v + 1
+                first = jnp.where(lane < 32, turned(one, block - 1), turned(one, block + 1))
+                second = jnp.where(lane < 96, turned(two, block - 1), turned(two, block + 1))
+                at = part * 256 + v * 128
+                e_refs[g][1 : n1 + 1, :, at : at + 128] = jnp.where(lane < 64, first, second)
+
+    def middle_layer(g):
         total = bias2
         for k in range(3):
             rows = pl.ds(off2 + k, n2)
             stack = []
-            for q in range(q0, q0 + 2):
-                parts = [h1_ref[rows, o * half : (o + 1) * half, q * 128 : (q + 1) * 128] for o in range(4)]
-                parts.append(e_ref[rows, :, q * 256 : (q + 1) * 256])
+            for part in range(2):
+                parts = [
+                    h1_refs[g][rows, o * half : (o + 1) * half, part * 128 : (part + 1) * 128] for o in range(4)
+                ]
+                parts.append(e_refs[g][rows, :, part * 256 : (part + 1) * 256])
                 stack.append(jnp.concatenate([p.reshape(n2 * half, p.shape[2]) for p in parts], axis=1))
             total = total + dot_nt(jnp.concatenate(stack, axis=0), w2_ref[k])
         total = jnp.maximum(total, 0.0).reshape(2, n2, half, 256).astype(BF16)
-        for q in range(q0, q0 + 2):
+        for part in range(2):
             for u in range(2):
-                h2_ref[1 : n2 + 1, u * half : (u + 1) * half, q * 128 : (q + 1) * 128] = total[q - q0, :, :, u * 128 : (u + 1) * 128]
-
-    off3 = rows_here * trow - start2
-    total = None
-    for k in range(3):
-        part = dot_nt(h2_ref[pl.ds(off3 + k, rows_here)].reshape(rows_here * WB, lanes), w3_ref[k])
-        total = part if total is None else total + part
+                h2_refs[g][1 : n2 + 1, u * half : (u + 1) * half, part * 128 : (part + 1) * 128] = total[
+                    part, :, :, u * 128 : (u + 1) * 128
+                ]
+
+    def last_layer(g):
+        parts = []
+        for k in range(3):
+            cells_in = h2_refs[g][pl.ds(off3 + k, rows_here)].reshape(rows_here * WB, 256)
+            parts.append(dot_nt(cells_in, w3_ref[k, :, g * 256 : (g + 1) * 256]))
+        return sum(parts)
+
+    for g in range(groups):
+        first_layer(g)
+    for g in range(groups):
+        borders(g)
+    for g in range(groups):
+        middle_layer(g)
+    total = sum(last_layer(g) for g in range(groups))
     for r in range(rows_here):
         for u in range(2):
             piece = total[(r * 2 + u) * half : (r * 2 + u + 1) * half]
@@ -401,12 +433,12 @@
         scratch_shapes=[
             pltpu.VMEM((8 + (grid_rows + 2) * PITCH, 128), F32),
             pltpu.VMEM((n1 + 2, WB, 256), BF16),
-            pltpu.VMEM((n1 + 2, 2 * WB, lanes), BF16),
-            pltpu.VMEM((n1 + 2, WB // 2, 2 * lanes), BF16),
-            pltpu.VMEM((n2 + 2, WB, lanes), BF16),
             pltpu.VMEM((rows_here * WB, 128), F32),
             pltpu.VMEM((rows_here * WB, 128), F32),
             pltpu.VMEM((rows_here * WB // 128, 256, 128), F32),
+            *[pltpu.VMEM((n1 + 2, 2 * WB, 256), BF16)] * (lanes // 256),
+            *[pltpu.VMEM((n1 + 2, WB // 2, 512), BF16)] * (lanes // 256),
+            *[pltpu.VMEM((n2 + 2, WB, 256), BF16)] * (lanes // 256),
         ],
         compiler_params=pltpu.CompilerParams(vmem_limit_bytes=VMEM_LIMIT),
         name="score",

time: 24 us -> 23.3 us (0.971)
  waiting for transfers between devices: 4.04 us -> 3.01 us
  Pallas kernels: 8.27 us -> 8.62 us
    ppermute x7, waiting for transfers between devices: 4.04 us -> 3.01 us  [swapped(): return lax.ppermute(values, axis, [(i, i ^ distance) for i in range(count)])]
    pallas_call x1 -> x2, Pallas kernels: 1.07 us -> 1.87 us  [the longest x1 1.03 us: spread(): weights = fetch(*(in_hbm(w) for w in weights))]
    pallas_call x1, Pallas kernels: 5.02 us -> 4.56 us  [per_device(): pl.pallas_call(functools.partial(score_kernel, rows_here, n1, n2), out_sh...]
  transfers between devices with their start and end apart: 7 -> 7, of which waited for: 3 -> 4; matrix products, arithmetic and copies ran while one was open for 1% -> 1% of each run, Pallas kernels for 14% -> 18%
where the time goes in v4:
time: 23.3 us; the launch traced here: 23.1 us
  starting transfers between devices  9.32 us (40%)
  Pallas kernels  8.62 us (37%)
  waiting for transfers between devices  3.01 us (13%)
  between operations  2.05 us (9%)
    ppermute x7, starting transfers between devices, swapped(): return lax.ppermute(values, axis, [(i, i ^ distance) for i in range(count)])  9.32 us
    pallas_call x1, Pallas kernels, per_device(): pl.pallas_call(functools.partial(score_kernel, rows_here, n1, n2), out_sh...  4.56 us
    ppermute x7, waiting for transfers between devices, swapped(): return lax.ppermute(values, axis, [(i, i ^ distance) for i in range(count)])  3.01 us
    pallas_call x1, Pallas kernels, per_device(): biased = lambda *taps: expand(*taps, in_hbm(b_first), in_hbm(b_middle))  2.19 us
    pallas_call x1, Pallas kernels, spread(): weights = fetch(*(in_hbm(w) for w in weights))  1.03 us
    pallas_call x1, Pallas kernels, spread(): pl.pallas_call(functools.partial(front_kernel, axis), out_shape=jax.Shape...  0.85 us
  transfers between devices with their start and end apart: 7, of which 4 were waited for; matrix products, arithmetic and copies ran while one was open for 1% of the time, Pallas kernels for 18%

profile of v4, /device:TPU:0, one launch (start us, length us, event | category | flops | bytes accessed | tf_op | source)
XLA Modules:
  0.0 23.1 jit_solution(9593088069488767304)
XLA Ops:
  0.0 0.0 copy-start
  0.0 0.5 %collective-permute-start = (bf16[64,1024]{1,0:T(8,128)(2,1)}, bf16[64,1024]{1,0:T(8,128)(2,1)S(1)}, u32[]{:S(2)}, u32[]{:S(2)}) collective-permute-start(bf16[64,1024]{1,0:T(8,128)(2,1)} %bitcast.23), channel_id=1, source_target_pairs={{0,2},{2,0},{4,6},{6,4},{8,10},{10,8},{12,14},{14,12},{16,18},{18,... | collective-permute-start | bytes 393224 | tf_op jit(solution)/shard_map/ppermute | solution.py:29
  0.5 0.8 %front.1 = bf16[32,1024]{1,0:T(8,128)(2,1)S(1)} custom-call(bf16[64,1024]{1,0:T(8,128)(2,1)} %bitcast.24), custom_call_target="tpu_custom_call" | custom-call | tf_op jit(solution)/shard_map/front/pallas_call | solution.py:63
  1.3 2.6 %collective-permute-start.5 = (bf16[512,512]{1,0:T(8,128)(2,1)}, bf16[512,512]{1,0:T(8,128)(2,1)S(1)}, u32[]{:S(2)}, u32[]{:S(2)}) collective-permute-start(bf16[512,512]{1,0:T(8,128)(2,1)} %bitcast.20), channel_id=1, source_target_pairs={{0,1},{1,0},{2,3},{3,2},{4,5},{5,4},{6,7},{7,6},{8,9},{9,8},{10,11... | collective-permute-start | bytes 1572872 | tf_op jit(solution)/shard_map/ppermute | solution.py:29
  4.6 0.0 collective-permute-done
  4.7 2.6 %collective-permute-start.1 = (bf16[32,1024]{1,0:T(8,128)(2,1)S(1)}, bf16[32,1024]{1,0:T(8,128)(2,1)S(1)}, u32[]{:S(2)}, u32[]{:S(2)}) collective-permute-start(bf16[32,1024]{1,0:T(8,128)(2,1)S(1)} %select_select_fusion), channel_id=1, source_target_pairs={{0,12},{2,14},{4,8},{6,10},{8,4},{10,6},{12,0},{14,2},{16,28},{18,... | collective-permute-start | bytes 196616 | tf_op jit(solution)/shard_map/ppermute | solution.py:29
  7.3 0.4 %collective-permute-start.2 = (bf16[32,1024]{1,0:T(8,128)(2,1)S(1)}, bf16[32,1024]{1,0:T(8,128)(2,1)S(1)}, u32[]{:S(2)}, u32[]{:S(2)}) collective-permute-start(bf16[32,1024]{1,0:T(8,128)(2,1)S(1)} %select_select_fusion), channel_id=1, source_target_pairs={{0,8},{2,10},{4,12},{6,14},{8,0},{10,2},{12,4},{14,6},{16,24},{18,... | collective-permute-start | bytes 196616 | tf_op jit(solution)/shard_map/ppermute | solution.py:29
  7.7 0.5 %collective-permute-start.3 = (bf16[32,1024]{1,0:T(8,128)(2,1)S(1)}, bf16[32,1024]{1,0:T(8,128)(2,1)S(1)}, u32[]{:S(2)}, u32[]{:S(2)}) collective-permute-start(bf16[32,1024]{1,0:T(8,128)(2,1)S(1)} %select_select_fusion), channel_id=1, source_target_pairs={{0,4},{2,6},{4,0},{6,2},{8,12},{10,14},{12,8},{14,10},{16,20},{18,... | collective-permute-start | bytes 196616 | tf_op jit(solution)/shard_map/ppermute | solution.py:29
  9.5 1.0 %fetch.1 = (bf16[27,3,16]{2,1,0:T(4,128)(2,1)S(1)}, bf16[81,16,16]{2,1,0:T(8,128)(2,1)S(1)}, bf16[27,3,16]{2,1,0:T(4,128)(2,1)S(1)}) custom-call(bf16[27,3,16]{2,1,0:T(4,128)(2,1)} %bitcast.25, bf16[81,16,16]{2,1,0:T(8,128)(2,1)} %bitcast.22, bf16[27,3,16]{2,1,0:T(4,128)(2,1)} %bitcast.26), custom_call_target="tpu_custom_call" | custom-call | tf_op jit(solution)/shard_map/fetch/pallas_call | solution.py:79
  10.6 0.0 collective-permute-done.1
  10.6 0.9 %collective-permute-done.2 = bf16[32,1024]{1,0:T(8,128)(2,1)S(1)} collective-permute-done((bf16[32,1024]{1,0:T(8,128)(2,1)S(1)}, bf16[32,1024]{1,0:T(8,128)(2,1)S(1)}, u32[]{:S(2)}, u32[]{:S(2)}) %collective-permute-start.2) | collective-permute-done | bytes 65568 | tf_op jit(solution)/shard_map/ppermute | solution.py:29
  11.5 0.4 %collective-permute-done.3 = bf16[32,1024]{1,0:T(8,128)(2,1)S(1)} collective-permute-done((bf16[32,1024]{1,0:T(8,128)(2,1)S(1)}, bf16[32,1024]{1,0:T(8,128)(2,1)S(1)}, u32[]{:S(2)}, u32[]{:S(2)}) %collective-permute-start.3) | collective-permute-done | bytes 65568 | tf_op jit(solution)/shard_map/ppermute | solution.py:29
  12.0 2.7 %collective-permute-start.4 = (bf16[32,1024]{1,0:T(8,128)(2,1)S(1)}, bf16[32,1024]{1,0:T(8,128)(2,1)S(1)}, u32[]{:S(2)}, u32[]{:S(2)}) collective-permute-start(bf16[32,1024]{1,0:T(8,128)(2,1)S(1)} %add_add_fusion), channel_id=1, source_target_pairs={{0,16},{2,18},{4,20},{6,22},{8,24},{10,26},{12,28},{14,30},{16,0},... | collective-permute-start | bytes 196616 | tf_op jit(solution)/shard_map/ppermute | solution.py:29
  14.6 2.2 %expand.1 = (bf16[3,1024,256]{2,1,0:T(8,128)(2,1)S(1)}, bf16[3,256,768]{2,1,0:T(8,128)(2,1)S(1)}, bf16[3,256,1024]{2,1,0:T(8,128)(2,1)S(1)}, f32[8,256]{1,0:T(8,128)S(1)}) custom-call(bf16[27,3,16]{2,1,0:T(4,128)(2,1)S(1)} %get-tuple-element.43.wf_ref, bf16[81,16,16]{2,1,0:T(8,128)(2,1)S(1)} %get-tuple-element.44.wm_ref, ...), custom_call_target="tpu_custom_call" | custom-call | tf_op jit(solution)/shard_map/expand/pallas_call | solution.py:424
  16.8 0.4 %collective-permute-done.4 = bf16[32,1024]{1,0:T(8,128)(2,1)S(1)} collective-permute-done((bf16[32,1024]{1,0:T(8,128)(2,1)S(1)}, bf16[32,1024]{1,0:T(8,128)(2,1)S(1)}, u32[]{:S(2)}, u32[]{:S(2)}) %collective-permute-start.4) | collective-permute-done | bytes 65568 | tf_op jit(solution)/shard_map/ppermute | solution.py:29
  17.2 0.1 iota.7.rest_ref
  17.3 0.0 collective-permute-start.6
  17.3 1.2 %collective-permute-done.6.qb_ref = bf16[32,1024]{1,0:T(8,128)(2,1)S(1)} collective-permute-done((bf16[32,1024]{1,0:T(8,128)(2,1)S(1)}, bf16[32,1024]{1,0:T(8,128)(2,1)S(1)}, u32[]{:S(2)}, u32[]{:S(2)}) %collective-permute-start.6) | collective-permute-done | bytes 65568 | tf_op jit(solution)/shard_map/ppermute | solution.py:29
  18.6 0.0 collective-permute-done.5.to_ref
  18.6 0.0 copy-done
  18.6 4.6 %score.1 = f32[1,64,256]{2,1,0:T(8,128)} custom-call(f32[8,128]{1,0:T(8,128)S(1)} %iota.7.rest_ref, f32[8,256]{1,0:T(8,128)S(1)} %get-tuple-element.51.rows_ref, bf16[512,512]{1,0:T(8,128)(2,1)S(1)} %bitcast.21, bf16[512,512]{1,0:T(8,128)(2,1)S(1)} %collective-permute-done.5.to_ref, bf16[32,1024]{1,0:T(8,128)(2,1)S(1)} %add.32.qa_ref, ...), custom_call_target="tpu_custom_call" | custom-call | tf_op jit(solution)/shard_map/score/pallas_call | solution.py:428
  (4 shorter events, 0.1 us)
Async XLA Ops:
  0.0 18.6 %copy-start = (bf16[1,512,512]{2,1,0:T(8,128)(2,1)S(1)}, bf16[1,512,512]{2,1,0:T(8,128)(2,1)}, u32[]{:S(2)}) copy-start(bf16[1,512,512]{2,1,0:T(8,128)(2,1)} %param.12) | copy-start | bytes 1572868
  0.0 4.6 %collective-permute-start = (bf16[64,1024]{1,0:T(8,128)(2,1)}, bf16[64,1024]{1,0:T(8,128)(2,1)S(1)}, u32[]{:S(2)}, u32[]{:S(2)}) collective-permute-start(bf16[64,1024]{1,0:T(8,128)(2,1)} %bitcast.23), channel_id=1, source_target_pairs={{0,2},{2,0},{4,6},{6,4},{8,10},{10,8},{12,14},{14,12},{16,18},{18,... | collective-permute-start | bytes 393224 | tf_op jit(solution)/shard_map/ppermute | solution.py:29
  1.3 17.3 %collective-permute-start.5 = (bf16[512,512]{1,0:T(8,128)(2,1)}, bf16[512,512]{1,0:T(8,128)(2,1)S(1)}, u32[]{:S(2)}, u32[]{:S(2)}) collective-permute-start(bf16[512,512]{1,0:T(8,128)(2,1)} %bitcast.20), channel_id=1, source_target_pairs={{0,1},{1,0},{2,3},{3,2},{4,5},{5,4},{6,7},{7,6},{8,9},{9,8},{10,11... | collective-permute-start | bytes 1572872 | tf_op jit(solution)/shard_map/ppermute | solution.py:29
  4.7 5.9 %collective-permute-start.1 = (bf16[32,1024]{1,0:T(8,128)(2,1)S(1)}, bf16[32,1024]{1,0:T(8,128)(2,1)S(1)}, u32[]{:S(2)}, u32[]{:S(2)}) collective-permute-start(bf16[32,1024]{1,0:T(8,128)(2,1)S(1)} %select_select_fusion), channel_id=1, source_target_pairs={{0,12},{2,14},{4,8},{6,10},{8,4},{10,6},{12,0},{14,2},{16,28},{18,... | collective-permute-start | bytes 196616 | tf_op jit(solution)/shard_map/ppermute | solution.py:29
  7.3 4.3 %collective-permute-start.2 = (bf16[32,1024]{1,0:T(8,128)(2,1)S(1)}, bf16[32,1024]{1,0:T(8,128)(2,1)S(1)}, u32[]{:S(2)}, u32[]{:S(2)}) collective-permute-start(bf16[32,1024]{1,0:T(8,128)(2,1)S(1)} %select_select_fusion), channel_id=1, source_target_pairs={{0,8},{2,10},{4,12},{6,14},{8,0},{10,2},{12,4},{14,6},{16,24},{18,... | collective-permute-start | bytes 196616 | tf_op jit(solution)/shard_map/ppermute | solution.py:29
  7.7 4.3 %collective-permute-start.3 = (bf16[32,1024]{1,0:T(8,128)(2,1)S(1)}, bf16[32,1024]{1,0:T(8,128)(2,1)S(1)}, u32[]{:S(2)}, u32[]{:S(2)}) collective-permute-start(bf16[32,1024]{1,0:T(8,128)(2,1)S(1)} %select_select_fusion), channel_id=1, source_target_pairs={{0,4},{2,6},{4,0},{6,2},{8,12},{10,14},{12,8},{14,10},{16,20},{18,... | collective-permute-start | bytes 196616 | tf_op jit(solution)/shard_map/ppermute | solution.py:29
  12.0 5.2 %collective-permute-start.4 = (bf16[32,1024]{1,0:T(8,128)(2,1)S(1)}, bf16[32,1024]{1,0:T(8,128)(2,1)S(1)}, u32[]{:S(2)}, u32[]{:S(2)}) collective-permute-start(bf16[32,1024]{1,0:T(8,128)(2,1)S(1)} %add_add_fusion), channel_id=1, source_target_pairs={{0,16},{2,18},{4,20},{6,22},{8,24},{10,26},{12,28},{14,30},{16,0},... | collective-permute-start | bytes 196616 | tf_op jit(solution)/shard_map/ppermute | solution.py:29
  17.3 1.3 %collective-permute-start.6 = (bf16[32,1024]{1,0:T(8,128)(2,1)S(1)}, bf16[32,1024]{1,0:T(8,128)(2,1)S(1)}, u32[]{:S(2)}, u32[]{:S(2)}) collective-permute-start(bf16[32,1024]{1,0:T(8,128)(2,1)S(1)} %add.32.qa_ref), channel_id=1, source_target_pairs={{0,2},{2,0},{4,6},{6,4},{8,10},{10,8},{12,14},{14,12},{16,18},{18,... | collective-permute-start | bytes 196616 | tf_op jit(solution)/shard_map/ppermute | solution.py:29

commit v5 on v4

--- a/solution.py
+++ b/solution.py
@@ -433,9 +433,9 @@
         scratch_shapes=[
             pltpu.VMEM((8 + (grid_rows + 2) * PITCH, 128), F32),
             pltpu.VMEM((n1 + 2, WB, 256), BF16),
-            pltpu.VMEM((rows_here * WB, 128), F32),
-            pltpu.VMEM((rows_here * WB, 128), F32),
-            pltpu.VMEM((rows_here * WB // 128, 256, 128), F32),
+            pltpu.VMEM((rows_here * WB + 8, 128), F32),
+            pltpu.VMEM((rows_here * WB + 8, 128), F32),
+            pltpu.VMEM((rows_here * WB // 128, 256 + 8, 128), F32),
             *[pltpu.VMEM((n1 + 2, 2 * WB, 256), BF16)] * (lanes // 256),
             *[pltpu.VMEM((n1 + 2, WB // 2, 512), BF16)] * (lanes // 256),
             *[pltpu.VMEM((n2 + 2, WB, 256), BF16)] * (lanes // 256),

time: 23.3 us -> 23.3 us (level)
  no operation moved by 1% of the time
where the time goes in v5:
time: 23.3 us; the launch traced here: 23.1 us
  starting transfers between devices  9.32 us (40%)
  Pallas kernels  8.62 us (37%)
  waiting for transfers between devices  3.01 us (13%)
  between operations  2.05 us (9%)
    ppermute x7, starting transfers between devices, swapped(): return lax.ppermute(values, axis, [(i, i ^ distance) for i in range(count)])  9.32 us
    pallas_call x1, Pallas kernels, per_device(): pl.pallas_call(functools.partial(score_kernel, rows_here, n1, n2), out_sh...  4.56 us
    ppermute x7, waiting for transfers between devices, swapped(): return lax.ppermute(values, axis, [(i, i ^ distance) for i in range(count)])  3.01 us
    pallas_call x1, Pallas kernels, per_device(): biased = lambda *taps: expand(*taps, in_hbm(b_first), in_hbm(b_middle))  2.19 us
    pallas_call x1, Pallas kernels, spread(): weights = fetch(*(in_hbm(w) for w in weights))  1.03 us
    pallas_call x1, Pallas kernels, spread(): pl.pallas_call(functools.partial(front_kernel, axis), out_shape=jax.Shape...  0.85 us
  transfers between devices with their start and end apart: 7, of which 4 were waited for; matrix products, arithmetic and copies ran while one was open for 1% of the time, Pallas kernels for 18%

profile of v5, /device:TPU:0, one launch (start us, length us, event | category | flops | bytes accessed | tf_op | source)
XLA Modules:
  0.0 23.1 jit_solution(11827442644250752429)
XLA Ops:
  0.0 0.0 copy-start
  0.0 0.5 %collective-permute-start = (bf16[64,1024]{1,0:T(8,128)(2,1)}, bf16[64,1024]{1,0:T(8,128)(2,1)S(1)}, u32[]{:S(2)}, u32[]{:S(2)}) collective-permute-start(bf16[64,1024]{1,0:T(8,128)(2,1)} %bitcast.23), channel_id=1, source_target_pairs={{0,2},{2,0},{4,6},{6,4},{8,10},{10,8},{12,14},{14,12},{16,18},{18,... | collective-permute-start | bytes 393224 | tf_op jit(solution)/shard_map/ppermute | solution.py:29
  0.5 0.8 %front.1 = bf16[32,1024]{1,0:T(8,128)(2,1)S(1)} custom-call(bf16[64,1024]{1,0:T(8,128)(2,1)} %bitcast.24), custom_call_target="tpu_custom_call" | custom-call | tf_op jit(solution)/shard_map/front/pallas_call | solution.py:63
  1.3 2.6 %collective-permute-start.5 = (bf16[512,512]{1,0:T(8,128)(2,1)}, bf16[512,512]{1,0:T(8,128)(2,1)S(1)}, u32[]{:S(2)}, u32[]{:S(2)}) collective-permute-start(bf16[512,512]{1,0:T(8,128)(2,1)} %bitcast.20), channel_id=1, source_target_pairs={{0,1},{1,0},{2,3},{3,2},{4,5},{5,4},{6,7},{7,6},{8,9},{9,8},{10,11... | collective-permute-start | bytes 1572872 | tf_op jit(solution)/shard_map/ppermute | solution.py:29
  4.6 0.0 collective-permute-done
  4.7 2.6 %collective-permute-start.1 = (bf16[32,1024]{1,0:T(8,128)(2,1)S(1)}, bf16[32,1024]{1,0:T(8,128)(2,1)S(1)}, u32[]{:S(2)}, u32[]{:S(2)}) collective-permute-start(bf16[32,1024]{1,0:T(8,128)(2,1)S(1)} %select_select_fusion), channel_id=1, source_target_pairs={{0,12},{2,14},{4,8},{6,10},{8,4},{10,6},{12,0},{14,2},{16,28},{18,... | collective-permute-start | bytes 196616 | tf_op jit(solution)/shard_map/ppermute | solution.py:29
  7.3 0.4 %collective-permute-start.2 = (bf16[32,1024]{1,0:T(8,128)(2,1)S(1)}, bf16[32,1024]{1,0:T(8,128)(2,1)S(1)}, u32[]{:S(2)}, u32[]{:S(2)}) collective-permute-start(bf16[32,1024]{1,0:T(8,128)(2,1)S(1)} %select_select_fusion), channel_id=1, source_target_pairs={{0,8},{2,10},{4,12},{6,14},{8,0},{10,2},{12,4},{14,6},{16,24},{18,... | collective-permute-start | bytes 196616 | tf_op jit(solution)/shard_map/ppermute | solution.py:29
  7.7 0.5 %collective-permute-start.3 = (bf16[32,1024]{1,0:T(8,128)(2,1)S(1)}, bf16[32,1024]{1,0:T(8,128)(2,1)S(1)}, u32[]{:S(2)}, u32[]{:S(2)}) collective-permute-start(bf16[32,1024]{1,0:T(8,128)(2,1)S(1)} %select_select_fusion), channel_id=1, source_target_pairs={{0,4},{2,6},{4,0},{6,2},{8,12},{10,14},{12,8},{14,10},{16,20},{18,... | collective-permute-start | bytes 196616 | tf_op jit(solution)/shard_map/ppermute | solution.py:29
  9.5 1.0 %fetch.1 = (bf16[27,3,16]{2,1,0:T(4,128)(2,1)S(1)}, bf16[81,16,16]{2,1,0:T(8,128)(2,1)S(1)}, bf16[27,3,16]{2,1,0:T(4,128)(2,1)S(1)}) custom-call(bf16[27,3,16]{2,1,0:T(4,128)(2,1)} %bitcast.25, bf16[81,16,16]{2,1,0:T(8,128)(2,1)} %bitcast.22, bf16[27,3,16]{2,1,0:T(4,128)(2,1)} %bitcast.26), custom_call_target="tpu_custom_call" | custom-call | tf_op jit(solution)/shard_map/fetch/pallas_call | solution.py:79
  10.6 0.0 collective-permute-done.1
  10.6 0.9 %collective-permute-done.2 = bf16[32,1024]{1,0:T(8,128)(2,1)S(1)} collective-permute-done((bf16[32,1024]{1,0:T(8,128)(2,1)S(1)}, bf16[32,1024]{1,0:T(8,128)(2,1)S(1)}, u32[]{:S(2)}, u32[]{:S(2)}) %collective-permute-start.2) | collective-permute-done | bytes 65568 | tf_op jit(solution)/shard_map/ppermute | solution.py:29
  11.5 0.4 %collective-permute-done.3 = bf16[32,1024]{1,0:T(8,128)(2,1)S(1)} collective-permute-done((bf16[32,1024]{1,0:T(8,128)(2,1)S(1)}, bf16[32,1024]{1,0:T(8,128)(2,1)S(1)}, u32[]{:S(2)}, u32[]{:S(2)}) %collective-permute-start.3) | collective-permute-done | bytes 65568 | tf_op jit(solution)/shard_map/ppermute | solution.py:29
  12.0 2.7 %collective-permute-start.4 = (bf16[32,1024]{1,0:T(8,128)(2,1)S(1)}, bf16[32,1024]{1,0:T(8,128)(2,1)S(1)}, u32[]{:S(2)}, u32[]{:S(2)}) collective-permute-start(bf16[32,1024]{1,0:T(8,128)(2,1)S(1)} %add_add_fusion), channel_id=1, source_target_pairs={{0,16},{2,18},{4,20},{6,22},{8,24},{10,26},{12,28},{14,30},{16,0},... | collective-permute-start | bytes 196616 | tf_op jit(solution)/shard_map/ppermute | solution.py:29
  14.6 2.2 %expand.1 = (bf16[3,1024,256]{2,1,0:T(8,128)(2,1)S(1)}, bf16[3,256,768]{2,1,0:T(8,128)(2,1)S(1)}, bf16[3,256,1024]{2,1,0:T(8,128)(2,1)S(1)}, f32[8,256]{1,0:T(8,128)S(1)}) custom-call(bf16[27,3,16]{2,1,0:T(4,128)(2,1)S(1)} %get-tuple-element.43.wf_ref, bf16[81,16,16]{2,1,0:T(8,128)(2,1)S(1)} %get-tuple-element.44.wm_ref, ...), custom_call_target="tpu_custom_call" | custom-call | tf_op jit(solution)/shard_map/expand/pallas_call | solution.py:424
  16.8 0.4 %collective-permute-done.4 = bf16[32,1024]{1,0:T(8,128)(2,1)S(1)} collective-permute-done((bf16[32,1024]{1,0:T(8,128)(2,1)S(1)}, bf16[32,1024]{1,0:T(8,128)(2,1)S(1)}, u32[]{:S(2)}, u32[]{:S(2)}) %collective-permute-start.4) | collective-permute-done | bytes 65568 | tf_op jit(solution)/shard_map/ppermute | solution.py:29
  17.2 0.1 iota.7.rest_ref
  17.3 0.0 collective-permute-start.6
  17.3 1.2 %collective-permute-done.6.qb_ref = bf16[32,1024]{1,0:T(8,128)(2,1)S(1)} collective-permute-done((bf16[32,1024]{1,0:T(8,128)(2,1)S(1)}, bf16[32,1024]{1,0:T(8,128)(2,1)S(1)}, u32[]{:S(2)}, u32[]{:S(2)}) %collective-permute-start.6) | collective-permute-done | bytes 65568 | tf_op jit(solution)/shard_map/ppermute | solution.py:29
  18.6 0.0 collective-permute-done.5.to_ref
  18.6 0.0 copy-done
  18.6 4.6 %score.1 = f32[1,64,256]{2,1,0:T(8,128)} custom-call(f32[8,128]{1,0:T(8,128)S(1)} %iota.7.rest_ref, f32[8,256]{1,0:T(8,128)S(1)} %get-tuple-element.51.rows_ref, bf16[512,512]{1,0:T(8,128)(2,1)S(1)} %bitcast.21, bf16[512,512]{1,0:T(8,128)(2,1)S(1)} %collective-permute-done.5.to_ref, bf16[32,1024]{1,0:T(8,128)(2,1)S(1)} %add.32.qa_ref, ...), custom_call_target="tpu_custom_call" | custom-call | tf_op jit(solution)/shard_map/score/pallas_call | solution.py:428
  (4 shorter events, 0.1 us)
Async XLA Ops:
  0.0 18.6 %copy-start = (bf16[1,512,512]{2,1,0:T(8,128)(2,1)S(1)}, bf16[1,512,512]{2,1,0:T(8,128)(2,1)}, u32[]{:S(2)}) copy-start(bf16[1,512,512]{2,1,0:T(8,128)(2,1)} %param.12) | copy-start | bytes 1572868
  0.0 4.6 %collective-permute-start = (bf16[64,1024]{1,0:T(8,128)(2,1)}, bf16[64,1024]{1,0:T(8,128)(2,1)S(1)}, u32[]{:S(2)}, u32[]{:S(2)}) collective-permute-start(bf16[64,1024]{1,0:T(8,128)(2,1)} %bitcast.23), channel_id=1, source_target_pairs={{0,2},{2,0},{4,6},{6,4},{8,10},{10,8},{12,14},{14,12},{16,18},{18,... | collective-permute-start | bytes 393224 | tf_op jit(solution)/shard_map/ppermute | solution.py:29
  1.3 17.3 %collective-permute-start.5 = (bf16[512,512]{1,0:T(8,128)(2,1)}, bf16[512,512]{1,0:T(8,128)(2,1)S(1)}, u32[]{:S(2)}, u32[]{:S(2)}) collective-permute-start(bf16[512,512]{1,0:T(8,128)(2,1)} %bitcast.20), channel_id=1, source_target_pairs={{0,1},{1,0},{2,3},{3,2},{4,5},{5,4},{6,7},{7,6},{8,9},{9,8},{10,11... | collective-permute-start | bytes 1572872 | tf_op jit(solution)/shard_map/ppermute | solution.py:29
  4.7 5.9 %collective-permute-start.1 = (bf16[32,1024]{1,0:T(8,128)(2,1)S(1)}, bf16[32,1024]{1,0:T(8,128)(2,1)S(1)}, u32[]{:S(2)}, u32[]{:S(2)}) collective-permute-start(bf16[32,1024]{1,0:T(8,128)(2,1)S(1)} %select_select_fusion), channel_id=1, source_target_pairs={{0,12},{2,14},{4,8},{6,10},{8,4},{10,6},{12,0},{14,2},{16,28},{18,... | collective-permute-start | bytes 196616 | tf_op jit(solution)/shard_map/ppermute | solution.py:29
  7.3 4.3 %collective-permute-start.2 = (bf16[32,1024]{1,0:T(8,128)(2,1)S(1)}, bf16[32,1024]{1,0:T(8,128)(2,1)S(1)}, u32[]{:S(2)}, u32[]{:S(2)}) collective-permute-start(bf16[32,1024]{1,0:T(8,128)(2,1)S(1)} %select_select_fusion), channel_id=1, source_target_pairs={{0,8},{2,10},{4,12},{6,14},{8,0},{10,2},{12,4},{14,6},{16,24},{18,... | collective-permute-start | bytes 196616 | tf_op jit(solution)/shard_map/ppermute | solution.py:29
  7.7 4.3 %collective-permute-start.3 = (bf16[32,1024]{1,0:T(8,128)(2,1)S(1)}, bf16[32,1024]{1,0:T(8,128)(2,1)S(1)}, u32[]{:S(2)}, u32[]{:S(2)}) collective-permute-start(bf16[32,1024]{1,0:T(8,128)(2,1)S(1)} %select_select_fusion), channel_id=1, source_target_pairs={{0,4},{2,6},{4,0},{6,2},{8,12},{10,14},{12,8},{14,10},{16,20},{18,... | collective-permute-start | bytes 196616 | tf_op jit(solution)/shard_map/ppermute | solution.py:29
  12.0 5.2 %collective-permute-start.4 = (bf16[32,1024]{1,0:T(8,128)(2,1)S(1)}, bf16[32,1024]{1,0:T(8,128)(2,1)S(1)}, u32[]{:S(2)}, u32[]{:S(2)}) collective-permute-start(bf16[32,1024]{1,0:T(8,128)(2,1)S(1)} %add_add_fusion), channel_id=1, source_target_pairs={{0,16},{2,18},{4,20},{6,22},{8,24},{10,26},{12,28},{14,30},{16,0},... | collective-permute-start | bytes 196616 | tf_op jit(solution)/shard_map/ppermute | solution.py:29
  17.3 1.3 %collective-permute-start.6 = (bf16[32,1024]{1,0:T(8,128)(2,1)S(1)}, bf16[32,1024]{1,0:T(8,128)(2,1)S(1)}, u32[]{:S(2)}, u32[]{:S(2)}) collective-permute-start(bf16[32,1024]{1,0:T(8,128)(2,1)S(1)} %add.32.qa_ref), channel_id=1, source_target_pairs={{0,2},{2,0},{4,6},{6,4},{8,10},{10,8},{12,14},{14,12},{16,18},{18,... | collective-permute-start | bytes 196616 | tf_op jit(solution)/shard_map/ppermute | solution.py:29

commit v6 on v5

--- a/solution.py
+++ b/solution.py
@@ -229,7 +229,7 @@
 
 def score_kernel(
     rows_here, n1, n2, rest_ref, rows_ref, tm_ref, to_ref, qa_ref, qb_ref, w1_ref, w2_ref, w3_ref,
-    out_ref, v_ref, x_ref, ya_ref, yb_ref, yt_ref, *layers,
+    out_ref, v_ref, x_ref, ya_ref, yb_ref, yt_ref, o_ref, sems, *layers,
 ):
     trow, bit = lax.axis_index("trow"), lax.axis_index("pair") % 2
     count = rest_ref[1:2, :]
@@ -370,6 +370,7 @@
     for v in range(here // 128):
         yt_ref[v, 0:128, :] = ya_ref[v * 128 : (v + 1) * 128, :].T
         yt_ref[v, 128:256, :] = yb_ref[v * 128 : (v + 1) * 128, :].T
+    copies = []
     lane = iota((WA, here), 1)
     keep = (rows_here * trow + lane // WB).astype(F32) < count[:, :1]
     for ra in range(2):
@@ -380,7 +381,12 @@
         before = jnp.where(lane % WB == 0, 0.0, pltpu.roll(parts[0], 1, 1))
         after = jnp.where(lane % WB == WB - 1, 0.0, pltpu.roll(parts[2], here - 1, 1))
         result = before + parts[1] + after + rest_ref[0:1, :1]
-        out_ref[0, ra * WA : (ra + 1) * WA, :] = jnp.where(keep, result, 0.0)
+        rows = slice(ra * WA, (ra + 1) * WA)
+        o_ref[rows, :] = jnp.where(keep, result, 0.0)
+        copies.append(pltpu.make_async_copy(o_ref.at[rows], out_ref.at[0, rows], sems.at[ra]))
+        copies[-1].start()
+    for copy in copies:
+        copy.wait()
 
 
 def per_device(
@@ -429,13 +435,15 @@
         functools.partial(score_kernel, rows_here, n1, n2),
         out_shape=jax.ShapeDtypeStruct((1, positions, rows_here * WB), F32),
         in_specs=[VMEM] * 9,
-        out_specs=VMEM,
+        out_specs=HBM,
         scratch_shapes=[
             pltpu.VMEM((8 + (grid_rows + 2) * PITCH, 128), F32),
             pltpu.VMEM((n1 + 2, WB, 256), BF16),
             pltpu.VMEM((rows_here * WB + 8, 128), F32),
             pltpu.VMEM((rows_here * WB + 8, 128), F32),
             pltpu.VMEM((rows_here * WB // 128, 256 + 8, 128), F32),
+            pltpu.VMEM((positions, rows_here * WB), F32),
+            pltpu.SemaphoreType.DMA((2,)),
             *[pltpu.VMEM((n1 + 2, 2 * WB, 256), BF16)] * (lanes // 256),
             *[pltpu.VMEM((n1 + 2, WB // 2, 512), BF16)] * (lanes // 256),
             *[pltpu.VMEM((n2 + 2, WB, 256), BF16)] * (lanes // 256),

time: 23.3 us -> 23.4 us (level)
  no operation moved by 1% of the time
where the time goes in v6:
time: 23.4 us; the launch traced here: 23.2 us
  starting transfers between devices  9.32 us (40%)
  Pallas kernels  8.65 us (37%)
  waiting for transfers between devices  3.01 us (13%)
  between operations  2.05 us (9%)
    ppermute x7, starting transfers between devices, swapped(): return lax.ppermute(values, axis, [(i, i ^ distance) for i in range(count)])  9.32 us
    pallas_call x1, Pallas kernels, per_device(): pl.pallas_call(functools.partial(score_kernel, rows_here, n1, n2), out_sh...  4.59 us
    ppermute x7, waiting for transfers between devices, swapped(): return lax.ppermute(values, axis, [(i, i ^ distance) for i in range(count)])  3.01 us
    pallas_call x1, Pallas kernels, per_device(): biased = lambda *taps: expand(*taps, in_hbm(b_first), in_hbm(b_middle))  2.19 us
    pallas_call x1, Pallas kernels, spread(): weights = fetch(*(in_hbm(w) for w in weights))  1.03 us
    pallas_call x1, Pallas kernels, spread(): pl.pallas_call(functools.partial(front_kernel, axis), out_shape=jax.Shape...  0.85 us
  transfers between devices with their start and end apart: 7, of which 4 were waited for; matrix products, arithmetic and copies ran while one was open for 1% of the time, Pallas kernels for 18%

profile of v6, /device:TPU:0, one launch (start us, length us, event | category | flops | bytes accessed | tf_op | source)
XLA Modules:
  0.0 23.2 jit_solution(1022173286217360218)
XLA Ops:
  0.0 0.0 copy-start
  0.0 0.5 %collective-permute-start = (bf16[64,1024]{1,0:T(8,128)(2,1)}, bf16[64,1024]{1,0:T(8,128)(2,1)S(1)}, u32[]{:S(2)}, u32[]{:S(2)}) collective-permute-start(bf16[64,1024]{1,0:T(8,128)(2,1)} %bitcast.23), channel_id=1, source_target_pairs={{0,2},{2,0},{4,6},{6,4},{8,10},{10,8},{12,14},{14,12},{16,18},{18,... | collective-permute-start | bytes 393224 | tf_op jit(solution)/shard_map/ppermute | solution.py:29
  0.5 0.8 %front.1 = bf16[32,1024]{1,0:T(8,128)(2,1)S(1)} custom-call(bf16[64,1024]{1,0:T(8,128)(2,1)} %bitcast.24), custom_call_target="tpu_custom_call" | custom-call | tf_op jit(solution)/shard_map/front/pallas_call | solution.py:63
  1.3 2.6 %collective-permute-start.5 = (bf16[512,512]{1,0:T(8,128)(2,1)}, bf16[512,512]{1,0:T(8,128)(2,1)S(1)}, u32[]{:S(2)}, u32[]{:S(2)}) collective-permute-start(bf16[512,512]{1,0:T(8,128)(2,1)} %bitcast.20), channel_id=1, source_target_pairs={{0,1},{1,0},{2,3},{3,2},{4,5},{5,4},{6,7},{7,6},{8,9},{9,8},{10,11... | collective-permute-start | bytes 1572872 | tf_op jit(solution)/shard_map/ppermute | solution.py:29
  4.6 0.0 collective-permute-done
  4.7 2.6 %collective-permute-start.1 = (bf16[32,1024]{1,0:T(8,128)(2,1)S(1)}, bf16[32,1024]{1,0:T(8,128)(2,1)S(1)}, u32[]{:S(2)}, u32[]{:S(2)}) collective-permute-start(bf16[32,1024]{1,0:T(8,128)(2,1)S(1)} %select_select_fusion), channel_id=1, source_target_pairs={{0,12},{2,14},{4,8},{6,10},{8,4},{10,6},{12,0},{14,2},{16,28},{18,... | collective-permute-start | bytes 196616 | tf_op jit(solution)/shard_map/ppermute | solution.py:29
  7.3 0.4 %collective-permute-start.2 = (bf16[32,1024]{1,0:T(8,128)(2,1)S(1)}, bf16[32,1024]{1,0:T(8,128)(2,1)S(1)}, u32[]{:S(2)}, u32[]{:S(2)}) collective-permute-start(bf16[32,1024]{1,0:T(8,128)(2,1)S(1)} %select_select_fusion), channel_id=1, source_target_pairs={{0,8},{2,10},{4,12},{6,14},{8,0},{10,2},{12,4},{14,6},{16,24},{18,... | collective-permute-start | bytes 196616 | tf_op jit(solution)/shard_map/ppermute | solution.py:29
  7.7 0.5 %collective-permute-start.3 = (bf16[32,1024]{1,0:T(8,128)(2,1)S(1)}, bf16[32,1024]{1,0:T(8,128)(2,1)S(1)}, u32[]{:S(2)}, u32[]{:S(2)}) collective-permute-start(bf16[32,1024]{1,0:T(8,128)(2,1)S(1)} %select_select_fusion), channel_id=1, source_target_pairs={{0,4},{2,6},{4,0},{6,2},{8,12},{10,14},{12,8},{14,10},{16,20},{18,... | collective-permute-start | bytes 196616 | tf_op jit(solution)/shard_map/ppermute | solution.py:29
  9.5 1.0 %fetch.1 = (bf16[27,3,16]{2,1,0:T(4,128)(2,1)S(1)}, bf16[81,16,16]{2,1,0:T(8,128)(2,1)S(1)}, bf16[27,3,16]{2,1,0:T(4,128)(2,1)S(1)}) custom-call(bf16[27,3,16]{2,1,0:T(4,128)(2,1)} %bitcast.25, bf16[81,16,16]{2,1,0:T(8,128)(2,1)} %bitcast.22, bf16[27,3,16]{2,1,0:T(4,128)(2,1)} %bitcast.26), custom_call_target="tpu_custom_call" | custom-call | tf_op jit(solution)/shard_map/fetch/pallas_call | solution.py:79
  10.6 0.0 collective-permute-done.1
  10.6 0.9 %collective-permute-done.2 = bf16[32,1024]{1,0:T(8,128)(2,1)S(1)} collective-permute-done((bf16[32,1024]{1,0:T(8,128)(2,1)S(1)}, bf16[32,1024]{1,0:T(8,128)(2,1)S(1)}, u32[]{:S(2)}, u32[]{:S(2)}) %collective-permute-start.2) | collective-permute-done | bytes 65568 | tf_op jit(solution)/shard_map/ppermute | solution.py:29
  11.5 0.4 %collective-permute-done.3 = bf16[32,1024]{1,0:T(8,128)(2,1)S(1)} collective-permute-done((bf16[32,1024]{1,0:T(8,128)(2,1)S(1)}, bf16[32,1024]{1,0:T(8,128)(2,1)S(1)}, u32[]{:S(2)}, u32[]{:S(2)}) %collective-permute-start.3) | collective-permute-done | bytes 65568 | tf_op jit(solution)/shard_map/ppermute | solution.py:29
  12.0 2.7 %collective-permute-start.4 = (bf16[32,1024]{1,0:T(8,128)(2,1)S(1)}, bf16[32,1024]{1,0:T(8,128)(2,1)S(1)}, u32[]{:S(2)}, u32[]{:S(2)}) collective-permute-start(bf16[32,1024]{1,0:T(8,128)(2,1)S(1)} %add_add_fusion), channel_id=1, source_target_pairs={{0,16},{2,18},{4,20},{6,22},{8,24},{10,26},{12,28},{14,30},{16,0},... | collective-permute-start | bytes 196616 | tf_op jit(solution)/shard_map/ppermute | solution.py:29
  14.6 2.2 %expand.1 = (bf16[3,1024,256]{2,1,0:T(8,128)(2,1)S(1)}, bf16[3,256,768]{2,1,0:T(8,128)(2,1)S(1)}, bf16[3,256,1024]{2,1,0:T(8,128)(2,1)S(1)}, f32[8,256]{1,0:T(8,128)S(1)}) custom-call(bf16[27,3,16]{2,1,0:T(4,128)(2,1)S(1)} %get-tuple-element.43.wf_ref, bf16[81,16,16]{2,1,0:T(8,128)(2,1)S(1)} %get-tuple-element.44.wm_ref, ...), custom_call_target="tpu_custom_call" | custom-call | tf_op jit(solution)/shard_map/expand/pallas_call | solution.py:430
  16.8 0.4 %collective-permute-done.4 = bf16[32,1024]{1,0:T(8,128)(2,1)S(1)} collective-permute-done((bf16[32,1024]{1,0:T(8,128)(2,1)S(1)}, bf16[32,1024]{1,0:T(8,128)(2,1)S(1)}, u32[]{:S(2)}, u32[]{:S(2)}) %collective-permute-start.4) | collective-permute-done | bytes 65568 | tf_op jit(solution)/shard_map/ppermute | solution.py:29
  17.2 0.1 iota.7.rest_ref
  17.3 0.0 collective-permute-start.6
  17.3 1.2 %collective-permute-done.6.qb_ref = bf16[32,1024]{1,0:T(8,128)(2,1)S(1)} collective-permute-done((bf16[32,1024]{1,0:T(8,128)(2,1)S(1)}, bf16[32,1024]{1,0:T(8,128)(2,1)S(1)}, u32[]{:S(2)}, u32[]{:S(2)}) %collective-permute-start.6) | collective-permute-done | bytes 65568 | tf_op jit(solution)/shard_map/ppermute | solution.py:29
  18.6 0.0 collective-permute-done.5.to_ref
  18.6 0.0 copy-done
  18.6 4.6 %score.1 = f32[1,64,256]{2,1,0:T(8,128)} custom-call(f32[8,128]{1,0:T(8,128)S(1)} %iota.7.rest_ref, f32[8,256]{1,0:T(8,128)S(1)} %get-tuple-element.51.rows_ref, bf16[512,512]{1,0:T(8,128)(2,1)S(1)} %bitcast.21, bf16[512,512]{1,0:T(8,128)(2,1)S(1)} %collective-permute-done.5.to_ref, bf16[32,1024]{1,0:T(8,128)(2,1)S(1)} %add.32.qa_ref, ...), custom_call_target="tpu_custom_call" | custom-call | tf_op jit(solution)/shard_map/score/pallas_call | solution.py:434
  (4 shorter events, 0.1 us)
Async XLA Ops:
  0.0 18.6 %copy-start = (bf16[1,512,512]{2,1,0:T(8,128)(2,1)S(1)}, bf16[1,512,512]{2,1,0:T(8,128)(2,1)}, u32[]{:S(2)}) copy-start(bf16[1,512,512]{2,1,0:T(8,128)(2,1)} %param.12) | copy-start | bytes 1572868
  0.0 4.6 %collective-permute-start = (bf16[64,1024]{1,0:T(8,128)(2,1)}, bf16[64,1024]{1,0:T(8,128)(2,1)S(1)}, u32[]{:S(2)}, u32[]{:S(2)}) collective-permute-start(bf16[64,1024]{1,0:T(8,128)(2,1)} %bitcast.23), channel_id=1, source_target_pairs={{0,2},{2,0},{4,6},{6,4},{8,10},{10,8},{12,14},{14,12},{16,18},{18,... | collective-permute-start | bytes 393224 | tf_op jit(solution)/shard_map/ppermute | solution.py:29
  1.3 17.3 %collective-permute-start.5 = (bf16[512,512]{1,0:T(8,128)(2,1)}, bf16[512,512]{1,0:T(8,128)(2,1)S(1)}, u32[]{:S(2)}, u32[]{:S(2)}) collective-permute-start(bf16[512,512]{1,0:T(8,128)(2,1)} %bitcast.20), channel_id=1, source_target_pairs={{0,1},{1,0},{2,3},{3,2},{4,5},{5,4},{6,7},{7,6},{8,9},{9,8},{10,11... | collective-permute-start | bytes 1572872 | tf_op jit(solution)/shard_map/ppermute | solution.py:29
  4.7 5.9 %collective-permute-start.1 = (bf16[32,1024]{1,0:T(8,128)(2,1)S(1)}, bf16[32,1024]{1,0:T(8,128)(2,1)S(1)}, u32[]{:S(2)}, u32[]{:S(2)}) collective-permute-start(bf16[32,1024]{1,0:T(8,128)(2,1)S(1)} %select_select_fusion), channel_id=1, source_target_pairs={{0,12},{2,14},{4,8},{6,10},{8,4},{10,6},{12,0},{14,2},{16,28},{18,... | collective-permute-start | bytes 196616 | tf_op jit(solution)/shard_map/ppermute | solution.py:29
  7.3 4.3 %collective-permute-start.2 = (bf16[32,1024]{1,0:T(8,128)(2,1)S(1)}, bf16[32,1024]{1,0:T(8,128)(2,1)S(1)}, u32[]{:S(2)}, u32[]{:S(2)}) collective-permute-start(bf16[32,1024]{1,0:T(8,128)(2,1)S(1)} %select_select_fusion), channel_id=1, source_target_pairs={{0,8},{2,10},{4,12},{6,14},{8,0},{10,2},{12,4},{14,6},{16,24},{18,... | collective-permute-start | bytes 196616 | tf_op jit(solution)/shard_map/ppermute | solution.py:29
  7.7 4.3 %collective-permute-start.3 = (bf16[32,1024]{1,0:T(8,128)(2,1)S(1)}, bf16[32,1024]{1,0:T(8,128)(2,1)S(1)}, u32[]{:S(2)}, u32[]{:S(2)}) collective-permute-start(bf16[32,1024]{1,0:T(8,128)(2,1)S(1)} %select_select_fusion), channel_id=1, source_target_pairs={{0,4},{2,6},{4,0},{6,2},{8,12},{10,14},{12,8},{14,10},{16,20},{18,... | collective-permute-start | bytes 196616 | tf_op jit(solution)/shard_map/ppermute | solution.py:29
  12.0 5.2 %collective-permute-start.4 = (bf16[32,1024]{1,0:T(8,128)(2,1)S(1)}, bf16[32,1024]{1,0:T(8,128)(2,1)S(1)}, u32[]{:S(2)}, u32[]{:S(2)}) collective-permute-start(bf16[32,1024]{1,0:T(8,128)(2,1)S(1)} %add_add_fusion), channel_id=1, source_target_pairs={{0,16},{2,18},{4,20},{6,22},{8,24},{10,26},{12,28},{14,30},{16,0},... | collective-permute-start | bytes 196616 | tf_op jit(solution)/shard_map/ppermute | solution.py:29
  17.3 1.3 %collective-permute-start.6 = (bf16[32,1024]{1,0:T(8,128)(2,1)S(1)}, bf16[32,1024]{1,0:T(8,128)(2,1)S(1)}, u32[]{:S(2)}, u32[]{:S(2)}) collective-permute-start(bf16[32,1024]{1,0:T(8,128)(2,1)S(1)} %add.32.qa_ref), channel_id=1, source_target_pairs={{0,2},{2,0},{4,6},{6,4},{8,10},{10,8},{12,14},{14,12},{16,18},{18,... | collective-permute-start | bytes 196616 | tf_op jit(solution)/shard_map/ppermute | solution.py:29
